TPU v7x, 128 devices: a whole 4x4x4 slice. The times are simulated.
128 devices in a mesh: dp: 4 (over z), verts: 32 (over y, x, core).
Axes of the slice: x: 4, y: 4, z: 4, core: 2. Of those that a mesh axis runs over, the one named last changes fastest.
Arguments:
- feats: bfloat16 [4, 32768, 512], P('dp', 'verts'), may hold values from -64 to 64
- weights: bfloat16 [4, 512, 512], replicated, may hold values from -0.25 to 0.25
- grad_out: bfloat16 [4, 32768, 512], P('dp', 'verts'), may hold values from -6 to 6
- neighbours: int32 [512, 8], replicated, may hold values from 0 to 511, as said below
- valid: int32 [512, 64], replicated, may hold values from 0 to 1, as said below
Outputs:
- attn_out: bfloat16 [4, 32768, 512], P('dp', 'verts')
- grad_feats: bfloat16 [4, 32768, 512], P('dp', 'verts')
- grad_weights: float32 [4, 512, 512], P(None, 'dp')
Inputs may be any that keep to these rules, and one draw needn't show every extreme that they name: `neighbours`: entry 0 of block b is b; entries 1 to 3 are other blocks of the same partition of 16 blocks (partition b // 16); entries 4 to 7 lie on four different other partitions. The blocks of one partition name exactly 2 distinct blocks of each other partition. A row names no block twice. `valid`: in each block the real vertices come first and are 32 or more.
All inputs are finite; a program needn't handle non-finite values.
Results may differ from a plain program's by a relative error of at most 0.0095.
The roundings to bfloat16 on the way count: a program that leaves them out, or rounds other values in their place, can miss the bound.
Values may be sent and summed in bfloat16 or wider, within the bound.
No kernel may reach another device: no remote copies, remote signals or barrier semaphores. Data moves between devices by JAX's collectives and lax.ppermute only.
A program may use at most 256 MiB of HBM per device.

v0:
```python
import functools
import math

import jax
import jax.numpy as jnp
from jax import lax
from jax.experimental import pallas as pl
from jax.experimental.pallas import tpu as pltpu
from jax.sharding import PartitionSpec as P

H = 8
BS = 64
NNB = 8
CAP = 2

ROWS = 1024
PAIR = 4
HALF = 256

NT = (((1,), (1,)), ((), ()))
TN = (((0,), (0,)), ((), ()))


def dot(a, b):
    return jnp.dot(a, b, preferred_element_type=jnp.float32)


def dot_nt(a, b):
    return lax.dot_general(a, b, NT, preferred_element_type=jnp.float32)


def dot_tn(a, b):
    return lax.dot_general(a, b, TN, preferred_element_type=jnp.float32)


def layer_kernel(
    scaling,
    entries,
    counts,
    far_hbm,
    own_k_hbm,
    own_v_hbm,
    wkv_hbm,
    q_hbm,
    u_hbm,
    diag_ref,
    att_hbm,
    gq_hbm,
    gk_hbm,
    gv_hbm,
    own_gk_hbm,
    own_gv_hbm,
    back_hbm,
    far_ref,
    wkv_ref,
    q_ref,
    u_ref,
    att_ref,
    gq_ref,
    keys,
    values,
    gkeys,
    gvalues,
    far_sem,
    in_sem,
    out_sem,
    grad_sem,
):
    parts = far_hbm.shape[0]
    remote = parts * CAP
    table, _, dim = keys.shape
    own = table - remote
    per = ROWS // BS
    half_parts = parts // per
    chunks = remote // per

    def far_copy(i):
        lanes = far_hbm.at[pl.ds(i % half_parts * per, per), i // half_parts]
        return pltpu.make_async_copy(lanes, far_ref.at[pl.ds(i * per, per)], far_sem.at[i])

    def back_copy(i):
        lanes = back_hbm.at[pl.ds(i % half_parts * per, per), i // half_parts]
        return pltpu.make_async_copy(far_ref.at[pl.ds(i * per, per)], lanes, far_sem.at[i])

    def grad_copies(i):
        at = pl.ds(i * per, per)
        return [
            pltpu.make_async_copy(keys.at[at], gk_hbm.at[at], grad_sem.at[0, i]),
            pltpu.make_async_copy(values.at[at], gv_hbm.at[at], grad_sem.at[1, i]),
        ]

    arrive = [
        pltpu.make_async_copy(wkv_hbm, wkv_ref, in_sem.at[0]),
        pltpu.make_async_copy(own_k_hbm, keys.at[pl.ds(remote, own)], in_sem.at[1]),
        pltpu.make_async_copy(own_v_hbm, values.at[pl.ds(remote, own)], in_sem.at[2]),
        pltpu.make_async_copy(q_hbm, q_ref, in_sem.at[3]),
        pltpu.make_async_copy(u_hbm, u_ref, in_sem.at[4]),
    ]
    arrive[0].start()
    for i in range(chunks):
        far_copy(i).start()
    for copy in arrive[1:]:
        copy.start()
    gkeys[pl.ds(remote, own)] = jnp.zeros((own, BS, dim), jnp.float32)
    gvalues[pl.ds(remote, own)] = jnp.zeros((own, BS, dim), jnp.float32)
    arrive[0].wait()

    def project(i, carry):
        first = pl.ds(i * per, per)
        far_copy(i).wait()
        both = dot(far_ref[first].reshape(ROWS, dim), wkv_ref[...]).astype(jnp.bfloat16)
        keys[first] = both[:, :dim].reshape(per, BS, dim)
        values[first] = both[:, dim:].reshape(per, BS, dim)
        gkeys[first] = jnp.zeros((per, BS, dim), jnp.float32)
        gvalues[first] = jnp.zeros((per, BS, dim), jnp.float32)
        return carry

    lax.fori_loop(0, chunks, project, 0)
    for copy in arrive[1:]:
        copy.wait()

    place = lax.broadcasted_iota(jnp.int32, (BS, HALF), 0)
    lane_head = lax.broadcasted_iota(jnp.int32, (BS, HALF), 1) // BS

    def attend(step, carry):
        diag = diag_ref[...]

        def first_half(sub, half):
            at = pl.ds(pl.multiple_of((step * PAIR + sub) * BS, BS), BS)
            cols = slice(half * HALF, (half + 1) * HALF)
            base = (step * PAIR + sub) * NNB
            ids = [entries[base + n] for n in range(NNB)]
            ends = [counts[base + n] for n in range(NNB)]
            queries = q_ref[at, cols] * jnp.bfloat16(scaling)
            qbd = jnp.concatenate([queries] * (HALF // BS), axis=0) * diag
            ubd = jnp.concatenate([u_ref[at, cols]] * (HALF // BS), axis=0) * diag
            k_all = jnp.concatenate([keys[i, :, cols] for i in ids], axis=0)
            v_all = jnp.concatenate([values[i, :, cols] for i in ids], axis=0)
            return at, cols, ids, ends, qbd, ubd, k_all, v_all, dot_nt(k_all, qbd), dot_nt(v_all, ubd)

        def second_half(at, cols, ids, ends, qbd, ubd, k_all, v_all, scores, dprob):
            scores = jnp.concatenate(
                [
                    jnp.where(place < ends[n], scores[n * BS : (n + 1) * BS], -1e30)
                    for n in range(NNB)
                ],
                axis=0,
            )
            top = jnp.max(scores, axis=0, keepdims=True)
            raised = jnp.exp(scores - top)
            probs = raised * (1.0 / jnp.sum(raised, axis=0, keepdims=True))
            probs_b = probs.astype(jnp.bfloat16)
            inner = jnp.sum(probs * dprob, axis=0, keepdims=True)
            dscore = (probs * (dprob - inner)).astype(jnp.bfloat16)
            grad_v = dot(probs_b, ubd)
            grad_k = dot(dscore, qbd)
            att_wide = dot_tn(probs_b, v_all)
            gq_wide = dot_tn(dscore, k_all)
            att = att_wide[:BS]
            gq = gq_wide[:BS]
            for h in range(1, HALF // BS):
                rows = slice(h * BS, (h + 1) * BS)
                att = jnp.where(lane_head == h, att_wide[rows], att)
                gq = jnp.where(lane_head == h, gq_wide[rows], gq)
            att_ref[at, cols] = att.astype(jnp.bfloat16)
            gq_ref[at, cols] = (gq * scaling).astype(jnp.bfloat16)
            for n in range(NNB):
                rows = slice(n * BS, (n + 1) * BS)
                gkeys[ids[n], :, cols] += grad_k[rows]
                gvalues[ids[n], :, cols] += grad_v[rows]

        todo = [(sub, half) for sub in range(PAIR) for half in range(dim // HALF)]
        held = first_half(*todo[0])
        for after in todo[1:] + [None]:
            ahead = first_half(*after) if after else None
            second_half(*held)
            held = ahead
        return carry

    lax.fori_loop(0, own // PAIR, attend, 0)

    leave = [
        pltpu.make_async_copy(att_ref, att_hbm, out_sem.at[0]),
        pltpu.make_async_copy(gq_ref, gq_hbm, out_sem.at[1]),
    ]
    last = pl.ds(remote, own)
    keys[last] = gkeys[last].astype(jnp.bfloat16)
    values[last] = gvalues[last].astype(jnp.bfloat16)
    leave += [
        pltpu.make_async_copy(keys.at[last], own_gk_hbm, out_sem.at[2]),
        pltpu.make_async_copy(values.at[last], own_gv_hbm, out_sem.at[3]),
    ]
    for copy in leave:
        copy.start()

    def send_back(i, carry):
        first = pl.ds(i * per, per)
        grad_k = gkeys[first].astype(jnp.bfloat16)
        grad_v = gvalues[first].astype(jnp.bfloat16)
        keys[first] = grad_k
        values[first] = grad_v
        for copy in grad_copies(i):
            copy.start()
        back = dot_nt(grad_k.reshape(ROWS, dim), wkv_ref[:, :dim]) + dot_nt(
            grad_v.reshape(ROWS, dim), wkv_ref[:, dim:]
        )
        far_ref[first] = back.astype(jnp.bfloat16).reshape(per, BS, dim)
        back_copy(i).start()
        return carry

    lax.fori_loop(0, chunks, send_back, 0)
    for i in range(chunks):
        leave += grad_copies(i) + [back_copy(i)]
    for copy in leave:
        copy.wait()


def layer_call(entries, counts, far, own_k, own_v, wkv, queries, ups, scaling):
    parts, _, _, dim = far.shape
    rows = queries.shape[0]
    own = rows // BS
    table = parts * CAP + own
    chunks = parts * CAP * BS // ROWS
    head = jnp.arange(HALF, dtype=jnp.int32) // BS
    diag = (head[:, None] == head[None, :]).astype(jnp.bfloat16)
    anywhere = pl.BlockSpec(memory_space=pl.ANY)
    return pl.pallas_call(
        functools.partial(layer_kernel, scaling),
        grid_spec=pltpu.PrefetchScalarGridSpec(
            num_scalar_prefetch=2,
            grid=(1,),
            in_specs=[anywhere] * 6 + [pl.BlockSpec((HALF, HALF), lambda i, *_: (0, 0))],
            out_specs=[anywhere] * 7,
            scratch_shapes=[
                pltpu.VMEM((parts * CAP, BS, dim), jnp.bfloat16),
                pltpu.VMEM((dim, 2 * dim), jnp.bfloat16),
                pltpu.VMEM((rows, dim), jnp.bfloat16),
                pltpu.VMEM((rows, dim), jnp.bfloat16),
                pltpu.VMEM((rows, dim), jnp.bfloat16),
                pltpu.VMEM((rows, dim), jnp.bfloat16),
                pltpu.VMEM((table, BS, dim), jnp.bfloat16),
                pltpu.VMEM((table, BS, dim), jnp.bfloat16),
                pltpu.VMEM((table, BS, dim), jnp.float32),
                pltpu.VMEM((table, BS, dim), jnp.float32),
                pltpu.SemaphoreType.DMA((chunks,)),
                pltpu.SemaphoreType.DMA((5,)),
                pltpu.SemaphoreType.DMA((4,)),
                pltpu.SemaphoreType.DMA((2, chunks)),
            ],
        ),
        out_shape=[
            jax.ShapeDtypeStruct((rows, dim), jnp.bfloat16),
            jax.ShapeDtypeStruct((rows, dim), jnp.bfloat16),
            jax.ShapeDtypeStruct((parts * CAP, BS, dim), jnp.bfloat16),
            jax.ShapeDtypeStruct((parts * CAP, BS, dim), jnp.bfloat16),
            jax.ShapeDtypeStruct((own, BS, dim), jnp.bfloat16),
            jax.ShapeDtypeStruct((own, BS, dim), jnp.bfloat16),
            jax.ShapeDtypeStruct(far.shape, jnp.bfloat16),
        ],
        compiler_params=pltpu.CompilerParams(vmem_limit_bytes=60 * 2**20),
    )(entries, counts, far, own_k, own_v, wkv, queries, ups, diag)


def weights_kernel(
    steps_far, core, far_ref, gk_ref, gv_ref, own_gk_ref, own_gv_ref, own_ref, gq_ref, att_ref, cot_ref, mine_ref, give_ref, terms
):
    step = pl.program_id(0)
    rows, dim = own_ref.shape

    @pl.when(step < steps_far)
    def _():
        far = far_ref[...].reshape(ROWS, dim)
        from_k = dot_tn(far, gk_ref[...].reshape(ROWS, dim))
        from_v = dot_tn(far, gv_ref[...].reshape(ROWS, dim))

        @pl.when(step == 0)
        def _():
            terms[2] = from_k
            terms[3] = from_v

        @pl.when(step > 0)
        def _():
            terms[2] += from_k
            terms[3] += from_v

    @pl.when(step == steps_far)
    def _():
        own = own_ref[...]
        terms[0] = dot_tn(own, gq_ref[...])
        terms[1] = dot_tn(att_ref[...], cot_ref[...])
        terms[2] += dot_tn(own, own_gk_ref[...])
        terms[3] += dot_tn(own, own_gv_ref[...])
        mine_ref[...] = terms[pl.ds(2 * core[0], 2)]
        give_ref[...] = terms[pl.ds(2 - 2 * core[0], 2)].astype(jnp.bfloat16)


def weights_call(core, far, grad_k, grad_v, own_gk, own_gv, own, grad_q, attended, cot):
    rows, dim = own.shape
    steps_far = far.shape[0] * CAP * BS // ROWS
    half = steps_far // CAP
    per = ROWS // BS

    def at_far(i, *_):
        chunk = jnp.minimum(i, steps_far - 1)
        return (chunk % half, chunk // half, 0, 0)

    def whole(shape):
        return pl.BlockSpec(shape, lambda i, *_: (0,) * len(shape), pipeline_mode=pl.Buffered(1))

    return pl.pallas_call(
        functools.partial(weights_kernel, steps_far),
        grid_spec=pltpu.PrefetchScalarGridSpec(
            num_scalar_prefetch=1,
            grid=(steps_far + 1,),
            in_specs=[
                pl.BlockSpec((per, None, BS, dim), at_far),
                pl.BlockSpec((per, BS, dim), lambda i, *_: (jnp.minimum(i, steps_far - 1), 0, 0)),
                pl.BlockSpec((per, BS, dim), lambda i, *_: (jnp.minimum(i, steps_far - 1), 0, 0)),
                whole((rows, dim)),
                whole((rows, dim)),
                whole((rows, dim)),
                whole((rows, dim)),
                whole((rows, dim)),
                whole((rows, dim)),
            ],
            out_specs=[whole((2, dim, dim)), whole((2, dim, dim))],
            scratch_shapes=[pltpu.VMEM((4, dim, dim), jnp.float32)],
        ),
        out_shape=[
            jax.ShapeDtypeStruct((2, dim, dim), jnp.float32),
            jax.ShapeDtypeStruct((2, dim, dim), jnp.bfloat16),
        ],
        compiler_params=pltpu.CompilerParams(vmem_limit_bytes=60 * 2**20),
        cost_estimate=pl.CostEstimate(flops=11 * 10**9, bytes_accessed=20 * 10**6, transcendentals=0),
    )(core, far, grad_k, grad_v, own_gk, own_gv, own, grad_q, attended, cot)


def combine_kernel(per, send_ref, base_ref, returned_ref, out_ref, acc):
    step = pl.program_id(0)

    @pl.when(step == 0)
    def _():
        acc[...] = base_ref[...]

    for i in range(per):
        for c in range(CAP):
            acc[send_ref[c, step * per + i]] += returned_ref[i, c].astype(jnp.float32)

    @pl.when(step == pl.num_programs(0) - 1)
    def _():
        out_ref[...] = acc[...].astype(jnp.bfloat16)


def combine_call(send, base, returned):
    blocks, _, dim = base.shape
    parts = returned.shape[0]
    per = 8
    return pl.pallas_call(
        functools.partial(combine_kernel, per),
        grid_spec=pltpu.PrefetchScalarGridSpec(
            num_scalar_prefetch=1,
            grid=(parts // per,),
            in_specs=[
                pl.BlockSpec((blocks, BS, dim), lambda i, *_: (0, 0, 0)),
                pl.BlockSpec((per, CAP, BS, dim), lambda i, *_: (i, 0, 0, 0)),
            ],
            out_specs=pl.BlockSpec((blocks, BS, dim), lambda i, *_: (0, 0, 0)),
            scratch_shapes=[pltpu.VMEM((blocks, BS, dim), jnp.float32)],
        ),
        out_shape=jax.ShapeDtypeStruct((blocks, BS, dim), jnp.bfloat16),
        compiler_params=pltpu.CompilerParams(vmem_limit_bytes=32 * 2**20),
    )(send, base, returned)


def over_cores_and_planes(mine, give, nparts):
    half = mine + lax.ppermute(give, "verts", [(v, v ^ 1) for v in range(nparts)]).astype(jnp.float32)
    planes = lax.axis_size("dp")
    here = lax.axis_index("dp")
    rows = half.shape[1] // planes
    total = lax.dynamic_slice_in_dim(half, here * rows, rows, 1)
    for d in range(1, planes):
        there = lax.dynamic_slice_in_dim(half, (here + d) % planes * rows, rows, 1)
        move = [(z, (z + d) % planes) for z in range(planes)]
        total += lax.ppermute(there.astype(jnp.bfloat16), "dp", move).astype(jnp.float32)
    return total


def moved(nparts, dx, dy):
    side = math.isqrt(nparts // 2)
    wide = nparts // side

    def go(i, d):
        return d(i) if callable(d) else (i + d) % side

    return [
        (v, go(v // wide, dy) * wide + go(v % wide // 2, dx) * 2 + v % 2) for v in range(nparts)
    ]


def ring_parts(value, nparts, along_x):
    side = math.isqrt(nparts // 2)
    moves = [moved(nparts, d, 0) if along_x else moved(nparts, 0, d) for d in range(1, side)]
    return [lax.ppermute(value, "verts", move) for move in moves]


def ring_sum(value, parts):
    one, two, three = [part.astype(jnp.float32) for part in parts]
    return ((value.astype(jnp.float32) + two) + (one + three)).astype(jnp.bfloat16)


def pair_sum(value, nparts, partner, along_x):
    move = moved(nparts, partner, 0) if along_x else moved(nparts, 0, partner)
    return value.astype(jnp.float32) + lax.ppermute(value, "verts", move).astype(jnp.float32)


def local(feats, weights, grad_out, neighbours, valid):
    nparts = lax.axis_size("verts")
    me = lax.axis_index("verts")
    _, rows, dim = feats.shape
    blocks = rows // BS
    scaling = 1.0 / math.sqrt(dim // H)
    part_ids = jnp.arange(nparts, dtype=jnp.int32)
    inputs_now = feats[0]
    cotangent = grad_out[0]
    w_kv = jnp.concatenate([weights[1], weights[2]], axis=1)

    theirs = neighbours.reshape(nparts, blocks * NNB)
    mine = (theirs // blocks == me) & (part_ids[:, None] != me)
    place = theirs % blocks
    low = jnp.min(jnp.where(mine, place, blocks), axis=1)
    high = jnp.max(jnp.where(mine, place, -1), axis=1)
    send = jnp.stack([low % blocks, jnp.maximum(high, 0)])

    lists = lax.dynamic_slice_in_dim(neighbours, me * blocks, blocks, 0).reshape(-1)
    owner = lists // blocks
    named = owner[:, None] == part_ids[None, :]
    lower = jnp.min(jnp.where(named, (lists % blocks)[:, None], blocks), axis=0)
    slot = (jnp.sum(jnp.where(named, lower[None, :], 0), axis=1) != lists % blocks).astype(jnp.int32)
    entries = jnp.where(owner == me, nparts * CAP + lists % blocks, slot * nparts + owner)
    counts = jnp.sum(valid, axis=1)[lists]

    far = lax.all_to_all(
        inputs_now.reshape(blocks, BS, dim)[send.T.reshape(-1)].reshape(nparts, CAP, BS, dim),
        "verts",
        split_axis=0,
        concat_axis=0,
        tiled=True,
    )

    queries = dot(inputs_now, weights[0]).astype(jnp.bfloat16)
    ups = dot_nt(cotangent, weights[3]).astype(jnp.bfloat16)
    own_k = dot(inputs_now, weights[1]).astype(jnp.bfloat16).reshape(blocks, BS, dim)
    own_v = dot(inputs_now, weights[2]).astype(jnp.bfloat16).reshape(blocks, BS, dim)

    attended, grad_q, grad_k, grad_v, own_gk, own_gv, back = layer_call(
        entries, counts, far, own_k, own_v, w_kv, queries, ups, scaling
    )
    own_gk, own_gv = own_gk.reshape(rows, dim), own_gv.reshape(rows, dim)
    returned = lax.all_to_all(back, "verts", split_axis=0, concat_axis=0, tiled=True)
    mine, give = weights_call(
        (me % 2).reshape(1),
        far,
        grad_k,
        grad_v,
        own_gk,
        own_gv,
        inputs_now,
        grad_q,
        attended,
        cotangent,
    )
    total = over_cores_and_planes(mine, give, nparts)
    attn_out = dot(attended, weights[3]).astype(jnp.bfloat16)
    base = dot_nt(grad_q, weights[0]) + dot_nt(own_gk, weights[1]) + dot_nt(own_gv, weights[2])
    total, attn_out, base = lax.optimization_barrier((total, attn_out, base))

    side = math.isqrt(nparts // 2)
    one, two = total[0].astype(jnp.bfloat16), total[1].astype(jnp.bfloat16)
    parts_one, parts_two, returned = lax.optimization_barrier(
        (ring_parts(one, nparts, True), ring_parts(two, nparts, False), returned)
    )
    one, two = ring_sum(one, parts_one), ring_sum(two, parts_two)
    grad_feats = combine_call(send, base.reshape(blocks, BS, dim), returned)
    one = pair_sum(one, nparts, lambda i: i ^ 1, False).astype(jnp.bfloat16)
    two = pair_sum(two, nparts, lambda i: i ^ 1, True).astype(jnp.bfloat16)
    one, two, grad_feats = lax.optimization_barrier((one, two, grad_feats))
    one = pair_sum(one, nparts, lambda i: side - 1 - i, False)
    two = pair_sum(two, nparts, lambda i: side - 1 - i, True)
    half = jnp.stack([one, two])
    other = lax.ppermute(half, "verts", [(v, v ^ 1) for v in range(nparts)])
    first = me % 2 == 0
    q_o = jnp.where(first, half, other)
    k_v = jnp.where(first, other, half)
    grad_weights = jnp.concatenate([q_o[:1], k_v, q_o[1:]], axis=0)
    return (attn_out[None], grad_feats.reshape(1, rows, dim), grad_weights)


def solution(mesh):
    in_specs = (P("dp", "verts", None), P(), P("dp", "verts", None), P(), P())
    out_specs = (P("dp", "verts", None), P("dp", "verts", None), P(None, "dp", None))
    return jax.shard_map(local, mesh=mesh, in_specs=in_specs, out_specs=out_specs, check_vma=False)
```

profile of v0, /device:TPU:1, one launch (start us, length us, event | category | flops | bytes accessed | tf_op | source)
XLA Modules:
  0.0 188.4 jit_solution(4438580279014357640)
XLA Ops:
  0.8 0.8 select_reduce_fusion.3
  2.3 4.0 %gather_fusion = bf16[64,64,512]{2,1,0:T(8,128)(2,1)} fusion(bf16[16,64,512]{2,1,0:T(8,128)(2,1)} %bitcast.66, s32[1024]{0:T(1024)S(1)} %pad_clamp_fusion.1), kind=kCustom, calls=%fused_computation | custom fusion | bytes 8388864 | tf_op jit(solution)/shard_map/gather | solution.py:443
  6.3 8.8 %all-to-all-start = ((bf16[32,2,64,512]{3,2,1,0:T(8,128)(2,1)}), bf16[32,2,64,512]{3,2,1,0:T(8,128)(2,1)}, u32[]{:S(2)}, u32[]{:S(2)}) async-start(bf16[32,2,64,512]{3,2,1,0:T(8,128)(2,1)} %bitcast.65), calls=%async_computation | async-start | bytes 8388608 | tf_op jit(solution)/shard_map/all_to_all | solution.py:442
  15.1 0.8 constant_dynamic-slice_fusion
  16.1 1.8 gather_fusion.1
  18.3 1.1 pad_maximum_fusion.wkv_hbm
  19.4 0.5 compare_select_fusion.5.entries
  19.9 0.7 compare_convert_fusion.diag_ref
  20.6 1.7 convolution_convert_fusion.4
  22.3 1.7 convolution_convert_fusion.3
  24.0 1.7 convolution_convert_fusion.2.q_hbm
  25.7 1.7 convolution_convert_fusion.1.u_hbm
  27.4 38.0 %all-to-all-done.far_hbm.far_ref = bf16[32,2,64,512]{3,2,1,0:T(8,128)(2,1)} async-done(((bf16[32,2,64,512]{3,2,1,0:T(8,128)(2,1)}), bf16[32,2,64,512]{3,2,1,0:T(8,128)(2,1)}, u32[]{:S(2)}, u32[]{:S(2)}) %all-to-all-start) | async-done | bytes 4194336 | tf_op jit(solution)/shard_map/all_to_all | solution.py:442
  65.3 37.5 %shard_map.76 = (bf16[1024,512]{1,0:T(8,128)(2,1)}, bf16[1024,512]{1,0:T(8,128)(2,1)}, bf16[64,64,512]{2,1,0:T(8,128)(2,1)}, bf16[64,64,512]{2,1,0:T(8,128)(2,1)...) custom-call(s32[128]{0:T(128)} %compare_select_fusion.5.entries, ...), custom_call_target="tpu_custom_call" | custom-call | tf_op jit(solution)/shard_map/pallas_call | solution.py:227
  102.8 8.2 %all-to-all-start.1 = ((bf16[32,2,64,512]{3,2,1,0:T(8,128)(2,1)}), bf16[32,2,64,512]{3,2,1,0:T(8,128)(2,1)}, u32[]{:S(2)}, u32[]{:S(2)}) async-start(bf16[32,2,64,512]{3,2,1,0:T(8,128)(2,1)} %get-tuple-element.35), calls=%async_computation.1 | async-start | bytes 8388608 | tf_op jit(solution)/shard_map/all_to_all | solution.py:459
  111.0 14.6 %shard_map.77 = (f32[2,512,512]{2,1,0:T(8,128)}, bf16[2,512,512]{2,1,0:T(8,128)(2,1)}) custom-call(s32[1]{0:T(128)} %bitcast.core, bf16[32,2,64,512]{3,2,1,0:T(8,128)(2,1)} %all-to-all-done.far_hbm.far_ref, bf16[64,64,512]{2,1,0:T(8,128)(2,1)} %get-tuple-element.25.gk_ref, bf16[64,64,512]{2,1,0:T(8,128)(2,1)} %get-tuple-element.26.gv_ref, ...), custom_call_target="tpu_custom_call" | custom-call | flops 11000000512 | bytes 20000000 | tf_op jit(solution)/shard_map/pallas_call | solution.py:310
  125.6 0.4 collective-permute-start
  126.1 0.7 fusion.2
  126.9 0.7 fusion.22
  127.6 0.8 copy-done.3
  128.5 0.3 copy-done.5
  128.7 0.8 add_add_fusion
  129.6 0.8 copy-done.4
  130.3 0.4 convert_add_fusion
  130.8 1.7 collective-permute-start.1
  132.5 3.3 %collective-permute-start.2 = (bf16[2,128,512]{2,1,0:T(8,128)(2,1)S(1)}, bf16[2,128,512]{2,1,0:T(8,128)(2,1)S(1)}, u32[]{:S(2)}, u32[]{:S(2)}) collective-permute-start(bf16[2,128,512]{2,1,0:T(8,128)(2,1)S(1)} %get-tuple-element.51), channel_id=1, source_target_pairs={{0,64},{32,96},{64,0},{96,32},{1,65},{33,97},{65,1},{97,33},{2,66}... | collective-permute-start | bytes 786440 | tf_op jit(solution)/shard_map/ppermute | solution.py:384
  135.8 0.7 collective-permute-start.3
  136.5 1.7 convolution_convert_fusion
  138.2 2.9 %collective-permute-done.1 = bf16[2,128,512]{2,1,0:T(8,128)(2,1)S(1)} collective-permute-done((bf16[2,128,512]{2,1,0:T(8,128)(2,1)S(1)}, bf16[2,128,512]{2,1,0:T(8,128)(2,1)S(1)}, u32[]{:S(2)}, u32[]{:S(2)}) %collective-permute-start.1) | collective-permute-done | bytes 262176 | tf_op jit(solution)/shard_map/ppermute | solution.py:384
  141.1 6.5 %collective-permute-done.2 = bf16[2,128,512]{2,1,0:T(8,128)(2,1)S(1)} collective-permute-done((bf16[2,128,512]{2,1,0:T(8,128)(2,1)S(1)}, bf16[2,128,512]{2,1,0:T(8,128)(2,1)S(1)}, u32[]{:S(2)}, u32[]{:S(2)}) %collective-permute-start.2) | collective-permute-done | bytes 262176 | tf_op jit(solution)/shard_map/ppermute | solution.py:384
  147.7 1.5 collective-permute-start.4
  149.2 2.4 %collective-permute-start.5 = (bf16[128,512]{1,0:T(8,128)(2,1)S(1)}, bf16[128,512]{1,0:T(8,128)(2,1)S(1)}, u32[]{:S(2)}, u32[]{:S(2)}) collective-permute-start(bf16[128,512]{1,0:T(8,128)(2,1)S(1)} %get-tuple-element.61), channel_id=1, source_target_pairs={{0,4},{1,5},{2,6},{3,7},{4,0},{5,1},{6,2},{7,3},{8,12},{9,13},{10,... | collective-permute-start | bytes 393224 | tf_op jit(solution)/shard_map/ppermute | solution.py:403
  151.7 1.2 collective-permute-start.6
  152.8 1.1 collective-permute-start.7
  153.9 2.6 %collective-permute-start.8 = (bf16[128,512]{1,0:T(8,128)(2,1)S(1)}, bf16[128,512]{1,0:T(8,128)(2,1)S(1)}, u32[]{:S(2)}, u32[]{:S(2)}) collective-permute-start(bf16[128,512]{1,0:T(8,128)(2,1)S(1)} %get-tuple-element.60), channel_id=1, source_target_pairs={{0,16},{1,17},{2,18},{3,19},{4,20},{5,21},{6,22},{7,23},{8,24},{9,... | collective-permute-start | bytes 393224 | tf_op jit(solution)/shard_map/ppermute | solution.py:403
  156.6 6.4 %collective-permute-done.4 = bf16[128,512]{1,0:T(8,128)(2,1)S(1)} collective-permute-done((bf16[128,512]{1,0:T(8,128)(2,1)S(1)}, bf16[128,512]{1,0:T(8,128)(2,1)S(1)}, u32[]{:S(2)}, u32[]{:S(2)}) %collective-permute-start.4) | collective-permute-done | bytes 131104 | tf_op jit(solution)/shard_map/ppermute | solution.py:403
  162.9 2.1 %collective-permute-start.9 = (bf16[128,512]{1,0:T(8,128)(2,1)S(1)}, bf16[128,512]{1,0:T(8,128)(2,1)S(1)}, u32[]{:S(2)}, u32[]{:S(2)}) collective-permute-start(bf16[128,512]{1,0:T(8,128)(2,1)S(1)} %get-tuple-element.60), channel_id=1, source_target_pairs={{0,24},{1,25},{2,26},{3,27},{4,28},{5,29},{6,30},{7,31},{8,0},{9,1... | collective-permute-start | bytes 393224 | tf_op jit(solution)/shard_map/ppermute | solution.py:403
  165.0 2.3 %collective-permute-done.5 = bf16[128,512]{1,0:T(8,128)(2,1)S(1)} collective-permute-done((bf16[128,512]{1,0:T(8,128)(2,1)S(1)}, bf16[128,512]{1,0:T(8,128)(2,1)S(1)}, u32[]{:S(2)}, u32[]{:S(2)}) %collective-permute-start.5) | collective-permute-done | bytes 131104 | tf_op jit(solution)/shard_map/ppermute | solution.py:403
  167.5 0.9 collective-permute-start.11
  168.5 1.4 collective-permute-start.10
  169.9 5.0 %shard_map.78 = bf16[16,64,512]{2,1,0:T(8,128)(2,1)} custom-call(s32[2,32]{1,0:T(2,128)S(1)} %get-tuple-element.62.send_ref, f32[16,64,512]{2,1,0:T(8,128)S(1)} %bitcast.64, bf16[32,2,64,512]{3,2,1,0:T(8,128)(2,1)} %all-to-all-done.1.returned_ref), custom_call_target="tpu_custom_call" | custom-call | tf_op jit(solution)/shard_map/pallas_call | solution.py:358
  175.0 1.6 collective-permute-start.12
  176.6 1.8 collective-permute-start.13
  178.4 1.7 collective-permute-done.12
  180.1 1.8 collective-permute-done.13
  182.0 3.7 %collective-permute-start.14 = (f32[2,128,512]{2,1,0:T(8,128)S(1)}, f32[2,128,512]{2,1,0:T(8,128)S(1)}, u32[]{:S(2)}, u32[]{:S(2)}) collective-permute-start(f32[2,128,512]{2,1,0:T(8,128)S(1)} %pad_maximum_fusion.2), channel_id=1, source_target_pairs={{0,1},{1,0},{2,3},{3,2},{4,5},{5,4},{6,7},{7,6},{8,9},{9,8},{10,11... | collective-permute-start | bytes 1572872 | tf_op jit(solution)/shard_map/ppermute | solution.py:490
  185.7 1.5 collective-permute-done.14
  187.4 1.1 pad_maximum_fusion.1
  (62 shorter events, 2.2 us)
Async XLA Ops:
  0.6 15.5 %copy-start = (s32[512,64]{0,1:T(8,128)S(1)}, s32[512,64]{0,1:T(8,128)}, u32[]{:S(2)}) copy-start(s32[512,64]{0,1:T(8,128)} %param.9) | copy-start | bytes 393220
  6.3 11.9 %copy-start.2 = (bf16[4,512,512]{2,1,0:T(8,128)(2,1)S(1)}, bf16[4,512,512]{2,1,0:T(8,128)(2,1)}, u32[]{:S(2)}) copy-start(bf16[4,512,512]{2,1,0:T(8,128)(2,1)} %param.6) | copy-start | bytes 6291460
  6.3 59.0 %all-to-all-start = ((bf16[32,2,64,512]{3,2,1,0:T(8,128)(2,1)}), bf16[32,2,64,512]{3,2,1,0:T(8,128)(2,1)}, u32[]{:S(2)}, u32[]{:S(2)}) async-start(bf16[32,2,64,512]{3,2,1,0:T(8,128)(2,1)} %bitcast.65), calls=%async_computation | async-start | bytes 8388608 | tf_op jit(solution)/shard_map/all_to_all | solution.py:442
  18.2 2.5 %copy-start.1 = (bf16[1,1024,512]{2,1,0:T(8,128)(2,1)S(1)}, bf16[1,1024,512]{2,1,0:T(8,128)(2,1)}, u32[]{:S(2)}) copy-start(bf16[1,1024,512]{2,1,0:T(8,128)(2,1)} %param.5) | copy-start | bytes 3145732
  24.0 1.7 copy-start.8
  102.8 64.6 %all-to-all-start.1 = ((bf16[32,2,64,512]{3,2,1,0:T(8,128)(2,1)}), bf16[32,2,64,512]{3,2,1,0:T(8,128)(2,1)}, u32[]{:S(2)}, u32[]{:S(2)}) async-start(bf16[32,2,64,512]{3,2,1,0:T(8,128)(2,1)} %get-tuple-element.35), calls=%async_computation.1 | async-start | bytes 8388608 | tf_op jit(solution)/shard_map/all_to_all | solution.py:459
  111.0 15.0 %copy-start.7 = (bf16[1024,512]{1,0:T(8,128)(2,1)S(1)}, bf16[1024,512]{1,0:T(8,128)(2,1)}, u32[]{:S(2)}) copy-start(bf16[1024,512]{1,0:T(8,128)(2,1)} %get-tuple-element.29.gq_ref) | copy-start | bytes 3145732
  125.6 1.2 copy-start.6
  125.6 3.9 %collective-permute-start = (bf16[2,512,512]{2,1,0:T(8,128)(2,1)}, bf16[2,512,512]{2,1,0:T(8,128)(2,1)S(1)}, u32[]{:S(2)}, u32[]{:S(2)}) collective-permute-start(bf16[2,512,512]{2,1,0:T(8,128)(2,1)} %get-tuple-element.32), channel_id=1, source_target_pairs={{0,1},{1,0},{2,3},{3,2},{4,5},{5,4},{6,7},{7,6},{8,9},{9,8},{10,11... | collective-permute-start | bytes 3145736 | tf_op jit(solution)/shard_map/ppermute | solution.py:376
  126.9 1.6 copy-start.3
  126.9 1.9 copy-start.5
  128.7 1.6 copy-start.4
  130.3 6.2 %copy-start.9 = (bf16[1024,512]{1,0:T(8,128)(2,1)S(1)}, bf16[1024,512]{1,0:T(8,128)(2,1)}, u32[]{:S(2)}) copy-start(bf16[1024,512]{1,0:T(8,128)(2,1)} %get-tuple-element.30.att_ref) | copy-start | bytes 3145732
  130.8 10.3 %collective-permute-start.1 = (bf16[2,128,512]{2,1,0:T(8,128)(2,1)S(1)}, bf16[2,128,512]{2,1,0:T(8,128)(2,1)S(1)}, u32[]{:S(2)}, u32[]{:S(2)}) collective-permute-start(bf16[2,128,512]{2,1,0:T(8,128)(2,1)S(1)} %get-tuple-element.49), channel_id=1, source_target_pairs={{0,32},{32,64},{64,96},{96,0},{1,33},{33,65},{65,97},{97,1},{2,34}... | collective-permute-start | bytes 786440 | tf_op jit(solution)/shard_map/ppermute | solution.py:384
  132.5 15.0 %collective-permute-start.2 = (bf16[2,128,512]{2,1,0:T(8,128)(2,1)S(1)}, bf16[2,128,512]{2,1,0:T(8,128)(2,1)S(1)}, u32[]{:S(2)}, u32[]{:S(2)}) collective-permute-start(bf16[2,128,512]{2,1,0:T(8,128)(2,1)S(1)} %get-tuple-element.51), channel_id=1, source_target_pairs={{0,64},{32,96},{64,0},{96,32},{1,65},{33,97},{65,1},{97,33},{2,66}... | collective-permute-start | bytes 786440 | tf_op jit(solution)/shard_map/ppermute | solution.py:384
  135.8 11.7 %collective-permute-start.3 = (bf16[2,128,512]{2,1,0:T(8,128)(2,1)S(1)}, bf16[2,128,512]{2,1,0:T(8,128)(2,1)S(1)}, u32[]{:S(2)}, u32[]{:S(2)}) collective-permute-start(bf16[2,128,512]{2,1,0:T(8,128)(2,1)S(1)} %get-tuple-element.50), channel_id=1, source_target_pairs={{0,96},{32,0},{64,32},{96,64},{1,97},{33,1},{65,33},{97,65},{2,98}... | collective-permute-start | bytes 786440 | tf_op jit(solution)/shard_map/ppermute | solution.py:384
  147.7 15.2 %collective-permute-start.4 = (bf16[128,512]{1,0:T(8,128)(2,1)S(1)}, bf16[128,512]{1,0:T(8,128)(2,1)S(1)}, u32[]{:S(2)}, u32[]{:S(2)}) collective-permute-start(bf16[128,512]{1,0:T(8,128)(2,1)S(1)} %get-tuple-element.61), channel_id=1, source_target_pairs={{0,2},{1,3},{2,4},{3,5},{4,6},{5,7},{6,0},{7,1},{8,10},{9,11},{10,... | collective-permute-start | bytes 393224 | tf_op jit(solution)/shard_map/ppermute | solution.py:403
  149.2 18.1 %collective-permute-start.5 = (bf16[128,512]{1,0:T(8,128)(2,1)S(1)}, bf16[128,512]{1,0:T(8,128)(2,1)S(1)}, u32[]{:S(2)}, u32[]{:S(2)}) collective-permute-start(bf16[128,512]{1,0:T(8,128)(2,1)S(1)} %get-tuple-element.61), channel_id=1, source_target_pairs={{0,4},{1,5},{2,6},{3,7},{4,0},{5,1},{6,2},{7,3},{8,12},{9,13},{10,... | collective-permute-start | bytes 393224 | tf_op jit(solution)/shard_map/ppermute | solution.py:403
  151.7 15.7 %collective-permute-start.6 = (bf16[128,512]{1,0:T(8,128)(2,1)S(1)}, bf16[128,512]{1,0:T(8,128)(2,1)S(1)}, u32[]{:S(2)}, u32[]{:S(2)}) collective-permute-start(bf16[128,512]{1,0:T(8,128)(2,1)S(1)} %get-tuple-element.61), channel_id=1, source_target_pairs={{0,6},{1,7},{2,0},{3,1},{4,2},{5,3},{6,4},{7,5},{8,14},{9,15},{10,... | collective-permute-start | bytes 393224 | tf_op jit(solution)/shard_map/ppermute | solution.py:403
  152.8 14.5 %collective-permute-start.7 = (bf16[128,512]{1,0:T(8,128)(2,1)S(1)}, bf16[128,512]{1,0:T(8,128)(2,1)S(1)}, u32[]{:S(2)}, u32[]{:S(2)}) collective-permute-start(bf16[128,512]{1,0:T(8,128)(2,1)S(1)} %get-tuple-element.60), channel_id=1, source_target_pairs={{0,8},{1,9},{2,10},{3,11},{4,12},{5,13},{6,14},{7,15},{8,16},{9,17... | collective-permute-start | bytes 393224 | tf_op jit(solution)/shard_map/ppermute | solution.py:403
  153.9 13.4 %collective-permute-start.8 = (bf16[128,512]{1,0:T(8,128)(2,1)S(1)}, bf16[128,512]{1,0:T(8,128)(2,1)S(1)}, u32[]{:S(2)}, u32[]{:S(2)}) collective-permute-start(bf16[128,512]{1,0:T(8,128)(2,1)S(1)} %get-tuple-element.60), channel_id=1, source_target_pairs={{0,16},{1,17},{2,18},{3,19},{4,20},{5,21},{6,22},{7,23},{8,24},{9,... | collective-permute-start | bytes 393224 | tf_op jit(solution)/shard_map/ppermute | solution.py:403
  162.9 4.4 %collective-permute-start.9 = (bf16[128,512]{1,0:T(8,128)(2,1)S(1)}, bf16[128,512]{1,0:T(8,128)(2,1)S(1)}, u32[]{:S(2)}, u32[]{:S(2)}) collective-permute-start(bf16[128,512]{1,0:T(8,128)(2,1)S(1)} %get-tuple-element.60), channel_id=1, source_target_pairs={{0,24},{1,25},{2,26},{3,27},{4,28},{5,29},{6,30},{7,31},{8,0},{9,1... | collective-permute-start | bytes 393224 | tf_op jit(solution)/shard_map/ppermute | solution.py:403
  167.5 7.3 %collective-permute-start.11 = (bf16[128,512]{1,0:T(8,128)(2,1)S(1)}, bf16[128,512]{1,0:T(8,128)(2,1)S(1)}, u32[]{:S(2)}, u32[]{:S(2)}) collective-permute-start(bf16[128,512]{1,0:T(8,128)(2,1)S(1)} %get-tuple-element.58), channel_id=1, source_target_pairs={{0,2},{1,3},{2,0},{3,1},{4,6},{5,7},{6,4},{7,5},{8,10},{9,11},{10,... | collective-permute-start | bytes 393224 | tf_op jit(solution)/shard_map/ppermute | solution.py:413
  168.5 6.4 %collective-permute-start.10 = (bf16[128,512]{1,0:T(8,128)(2,1)S(1)}, bf16[128,512]{1,0:T(8,128)(2,1)S(1)}, u32[]{:S(2)}, u32[]{:S(2)}) collective-permute-start(bf16[128,512]{1,0:T(8,128)(2,1)S(1)} %get-tuple-element.59), channel_id=1, source_target_pairs={{0,8},{1,9},{2,10},{3,11},{4,12},{5,13},{6,14},{7,15},{8,0},{9,1},... | collective-permute-start | bytes 393224 | tf_op jit(solution)/shard_map/ppermute | solution.py:413
  175.0 5.1 %collective-permute-start.12 = (bf16[128,512]{1,0:T(8,128)(2,1)S(1)}, bf16[128,512]{1,0:T(8,128)(2,1)S(1)}, u32[]{:S(2)}, u32[]{:S(2)}) collective-permute-start(bf16[128,512]{1,0:T(8,128)(2,1)S(1)} %add_convert_fusion.2), channel_id=1, source_target_pairs={{0,24},{1,25},{2,26},{3,27},{4,28},{5,29},{6,30},{7,31},{8,16},{9,... | collective-permute-start | bytes 393224 | tf_op jit(solution)/shard_map/ppermute | solution.py:413
  176.6 5.3 %collective-permute-start.13 = (bf16[128,512]{1,0:T(8,128)(2,1)S(1)}, bf16[128,512]{1,0:T(8,128)(2,1)S(1)}, u32[]{:S(2)}, u32[]{:S(2)}) collective-permute-start(bf16[128,512]{1,0:T(8,128)(2,1)S(1)} %add_convert_fusion), channel_id=1, source_target_pairs={{0,6},{1,7},{2,4},{3,5},{4,2},{5,3},{6,0},{7,1},{8,14},{9,15},{10,... | collective-permute-start | bytes 393224 | tf_op jit(solution)/shard_map/ppermute | solution.py:413
  182.0 5.2 %collective-permute-start.14 = (f32[2,128,512]{2,1,0:T(8,128)S(1)}, f32[2,128,512]{2,1,0:T(8,128)S(1)}, u32[]{:S(2)}, u32[]{:S(2)}) collective-permute-start(f32[2,128,512]{2,1,0:T(8,128)S(1)} %pad_maximum_fusion.2), channel_id=1, source_target_pairs={{0,1},{1,0},{2,3},{3,2},{4,5},{5,4},{6,7},{7,6},{8,9},{9,8},{10,11... | collective-permute-start | bytes 1572872 | tf_op jit(solution)/shard_map/ppermute | solution.py:490
where the time goes:
time: 189 us; the launch traced here: 188 us
  waiting for transfers between devices  61.1 us (32%)
  Pallas kernels  57.1 us (30%)
  starting transfers between devices  43.5 us (23%)
  matrix products  10.7 us (6%)
  local copies, waits for them, and re-layouts  9.54 us (5%)
  other arithmetic  5.6 us (3%)
    all_to_all x1, waiting for transfers between devices, local(): lax.all_to_all(inputs_now.reshape(blocks, BS, dim)[send.T.reshape(-1)].re...  38 us
    pallas_call x1, Pallas kernels, layer_call(): pl.pallas_call(functools.partial(layer_kernel, scaling), grid_spec=pltpu....  37.5 us
    pallas_call x1, Pallas kernels, weights_call(): pl.pallas_call(functools.partial(weights_kernel, steps_far), grid_spec=pl...  14.6 us
    ppermute x6, starting transfers between devices, ring_parts(): return [lax.ppermute(value, 'verts', move) for move in moves]  10.9 us
    ppermute x3, waiting for transfers between devices, over_cores_and_planes(): lax.ppermute(there.astype(jnp.bfloat16), 'dp', move).astype(jnp.float32)  9.32 us
    all_to_all x1, starting transfers between devices, local(): lax.all_to_all(inputs_now.reshape(blocks, BS, dim)[send.T.reshape(-1)].re...  8.78 us
    ppermute x6, waiting for transfers between devices, ring_parts(): return [lax.ppermute(value, 'verts', move) for move in moves]  8.77 us
    all_to_all x1, starting transfers between devices, local(): lax.all_to_all(back, 'verts', split_axis=0, concat_axis=0, tiled=True)  8.16 us
  transfers between devices with their start and end apart: 17, of which 8 were waited for; matrix products, arithmetic and copies ran while one was open for 9% of the time, Pallas kernels for 10%

commit v1 on v0

--- a/solution.py
+++ b/solution.py
@@ -486,11 +486,11 @@
     one, two, grad_feats = lax.optimization_barrier((one, two, grad_feats))
     one = pair_sum(one, nparts, lambda i: side - 1 - i, False)
     two = pair_sum(two, nparts, lambda i: side - 1 - i, True)
-    half = jnp.stack([one, two])
+    half = jnp.stack([one, two]).astype(jnp.bfloat16)
     other = lax.ppermute(half, "verts", [(v, v ^ 1) for v in range(nparts)])
     first = me % 2 == 0
-    q_o = jnp.where(first, half, other)
-    k_v = jnp.where(first, other, half)
+    q_o = jnp.where(first, half, other).astype(jnp.float32)
+    k_v = jnp.where(first, other, half).astype(jnp.float32)
     grad_weights = jnp.concatenate([q_o[:1], k_v, q_o[1:]], axis=0)
     return (attn_out[None], grad_feats.reshape(1, rows, dim), grad_weights)
 

time: 189 us -> 188 us (level)
  no operation moved by 1% of the time
where the time goes in v1:
time: 188 us
  waiting for transfers between devices  60.7 us (32%)
  Pallas kernels  57.1 us (30%)
  starting transfers between devices  43.5 us (23%)
  matrix products  10.7 us (6%)
  local copies, waits for them, and re-layouts  9.54 us (5%)
  other arithmetic  5.58 us (3%)
    all_to_all x1, waiting for transfers between devices, local(): lax.all_to_all(inputs_now.reshape(blocks, BS, dim)[send.T.reshape(-1)].re...  38 us
    pallas_call x1, Pallas kernels, layer_call(): pl.pallas_call(functools.partial(layer_kernel, scaling), grid_spec=pltpu....  37.5 us
    pallas_call x1, Pallas kernels, weights_call(): pl.pallas_call(functools.partial(weights_kernel, steps_far), grid_spec=pl...  14.6 us
    ppermute x6, starting transfers between devices, ring_parts(): return [lax.ppermute(value, 'verts', move) for move in moves]  10.9 us
    ppermute x3, waiting for transfers between devices, over_cores_and_planes(): lax.ppermute(there.astype(jnp.bfloat16), 'dp', move).astype(jnp.float32)  9.32 us
    all_to_all x1, starting transfers between devices, local(): lax.all_to_all(inputs_now.reshape(blocks, BS, dim)[send.T.reshape(-1)].re...  8.78 us
    ppermute x6, waiting for transfers between devices, ring_parts(): return [lax.ppermute(value, 'verts', move) for move in moves]  8.77 us
    all_to_all x1, starting transfers between devices, local(): lax.all_to_all(back, 'verts', split_axis=0, concat_axis=0, tiled=True)  8.16 us
  transfers between devices with their start and end apart: 17, of which 8 were waited for; matrix products, arithmetic and copies ran while one was open for 9% of the time, Pallas kernels for 10%

profile of v1, /device:TPU:1, one launch (start us, length us, event | category | flops | bytes accessed | tf_op | source)
XLA Modules:
  0.0 188.0 jit_solution(13965352539759189770)
XLA Ops:
  0.8 0.8 select_reduce_fusion.3
  2.3 4.0 %gather_fusion = bf16[64,64,512]{2,1,0:T(8,128)(2,1)} fusion(bf16[16,64,512]{2,1,0:T(8,128)(2,1)} %bitcast.66, s32[1024]{0:T(1024)S(1)} %pad_clamp_fusion.1), kind=kCustom, calls=%fused_computation | custom fusion | bytes 8388864 | tf_op jit(solution)/shard_map/gather | solution.py:443
  6.3 8.8 %all-to-all-start = ((bf16[32,2,64,512]{3,2,1,0:T(8,128)(2,1)}), bf16[32,2,64,512]{3,2,1,0:T(8,128)(2,1)}, u32[]{:S(2)}, u32[]{:S(2)}) async-start(bf16[32,2,64,512]{3,2,1,0:T(8,128)(2,1)} %bitcast.65), calls=%async_computation | async-start | bytes 8388608 | tf_op jit(solution)/shard_map/all_to_all | solution.py:442
  15.1 0.8 constant_dynamic-slice_fusion
  16.1 1.8 gather_fusion.1
  18.3 1.1 pad_maximum_fusion.wkv_hbm
  19.4 0.5 compare_select_fusion.5.entries
  19.9 0.7 compare_convert_fusion.diag_ref
  20.6 1.7 convolution_convert_fusion.4
  22.3 1.7 convolution_convert_fusion.3
  24.0 1.7 convolution_convert_fusion.2.q_hbm
  25.7 1.7 convolution_convert_fusion.1.u_hbm
  27.4 38.0 %all-to-all-done.far_hbm.far_ref = bf16[32,2,64,512]{3,2,1,0:T(8,128)(2,1)} async-done(((bf16[32,2,64,512]{3,2,1,0:T(8,128)(2,1)}), bf16[32,2,64,512]{3,2,1,0:T(8,128)(2,1)}, u32[]{:S(2)}, u32[]{:S(2)}) %all-to-all-start) | async-done | bytes 4194336 | tf_op jit(solution)/shard_map/all_to_all | solution.py:442
  65.3 37.5 %shard_map.76 = (bf16[1024,512]{1,0:T(8,128)(2,1)}, bf16[1024,512]{1,0:T(8,128)(2,1)}, bf16[64,64,512]{2,1,0:T(8,128)(2,1)}, bf16[64,64,512]{2,1,0:T(8,128)(2,1)...) custom-call(s32[128]{0:T(128)} %compare_select_fusion.5.entries, ...), custom_call_target="tpu_custom_call" | custom-call | tf_op jit(solution)/shard_map/pallas_call | solution.py:227
  102.8 8.2 %all-to-all-start.1 = ((bf16[32,2,64,512]{3,2,1,0:T(8,128)(2,1)}), bf16[32,2,64,512]{3,2,1,0:T(8,128)(2,1)}, u32[]{:S(2)}, u32[]{:S(2)}) async-start(bf16[32,2,64,512]{3,2,1,0:T(8,128)(2,1)} %get-tuple-element.35), calls=%async_computation.1 | async-start | bytes 8388608 | tf_op jit(solution)/shard_map/all_to_all | solution.py:459
  111.0 14.6 %shard_map.77 = (f32[2,512,512]{2,1,0:T(8,128)}, bf16[2,512,512]{2,1,0:T(8,128)(2,1)}) custom-call(s32[1]{0:T(128)} %bitcast.core, bf16[32,2,64,512]{3,2,1,0:T(8,128)(2,1)} %all-to-all-done.far_hbm.far_ref, bf16[64,64,512]{2,1,0:T(8,128)(2,1)} %get-tuple-element.25.gk_ref, bf16[64,64,512]{2,1,0:T(8,128)(2,1)} %get-tuple-element.26.gv_ref, ...), custom_call_target="tpu_custom_call" | custom-call | flops 11000000512 | bytes 20000000 | tf_op jit(solution)/shard_map/pallas_call | solution.py:310
  125.6 0.4 collective-permute-start
  126.1 0.7 fusion.2
  126.9 0.7 fusion.24
  127.6 0.8 copy-done.3
  128.5 0.3 copy-done.5
  128.7 0.8 add_add_fusion
  129.6 0.8 copy-done.4
  130.3 0.4 convert_add_fusion
  130.8 1.7 collective-permute-start.1
  132.5 3.3 %collective-permute-start.2 = (bf16[2,128,512]{2,1,0:T(8,128)(2,1)S(1)}, bf16[2,128,512]{2,1,0:T(8,128)(2,1)S(1)}, u32[]{:S(2)}, u32[]{:S(2)}) collective-permute-start(bf16[2,128,512]{2,1,0:T(8,128)(2,1)S(1)} %get-tuple-element.51), channel_id=1, source_target_pairs={{0,64},{32,96},{64,0},{96,32},{1,65},{33,97},{65,1},{97,33},{2,66}... | collective-permute-start | bytes 786440 | tf_op jit(solution)/shard_map/ppermute | solution.py:384
  135.8 0.7 collective-permute-start.3
  136.5 1.7 convolution_convert_fusion
  138.2 2.9 %collective-permute-done.1 = bf16[2,128,512]{2,1,0:T(8,128)(2,1)S(1)} collective-permute-done((bf16[2,128,512]{2,1,0:T(8,128)(2,1)S(1)}, bf16[2,128,512]{2,1,0:T(8,128)(2,1)S(1)}, u32[]{:S(2)}, u32[]{:S(2)}) %collective-permute-start.1) | collective-permute-done | bytes 262176 | tf_op jit(solution)/shard_map/ppermute | solution.py:384
  141.1 6.5 %collective-permute-done.2 = bf16[2,128,512]{2,1,0:T(8,128)(2,1)S(1)} collective-permute-done((bf16[2,128,512]{2,1,0:T(8,128)(2,1)S(1)}, bf16[2,128,512]{2,1,0:T(8,128)(2,1)S(1)}, u32[]{:S(2)}, u32[]{:S(2)}) %collective-permute-start.2) | collective-permute-done | bytes 262176 | tf_op jit(solution)/shard_map/ppermute | solution.py:384
  147.7 1.5 collective-permute-start.4
  149.2 2.4 %collective-permute-start.5 = (bf16[128,512]{1,0:T(8,128)(2,1)S(1)}, bf16[128,512]{1,0:T(8,128)(2,1)S(1)}, u32[]{:S(2)}, u32[]{:S(2)}) collective-permute-start(bf16[128,512]{1,0:T(8,128)(2,1)S(1)} %get-tuple-element.61), channel_id=1, source_target_pairs={{0,4},{1,5},{2,6},{3,7},{4,0},{5,1},{6,2},{7,3},{8,12},{9,13},{10,... | collective-permute-start | bytes 393224 | tf_op jit(solution)/shard_map/ppermute | solution.py:403
  151.7 1.2 collective-permute-start.6
  152.8 1.1 collective-permute-start.7
  153.9 2.6 %collective-permute-start.8 = (bf16[128,512]{1,0:T(8,128)(2,1)S(1)}, bf16[128,512]{1,0:T(8,128)(2,1)S(1)}, u32[]{:S(2)}, u32[]{:S(2)}) collective-permute-start(bf16[128,512]{1,0:T(8,128)(2,1)S(1)} %get-tuple-element.60), channel_id=1, source_target_pairs={{0,16},{1,17},{2,18},{3,19},{4,20},{5,21},{6,22},{7,23},{8,24},{9,... | collective-permute-start | bytes 393224 | tf_op jit(solution)/shard_map/ppermute | solution.py:403
  156.6 6.4 %collective-permute-done.4 = bf16[128,512]{1,0:T(8,128)(2,1)S(1)} collective-permute-done((bf16[128,512]{1,0:T(8,128)(2,1)S(1)}, bf16[128,512]{1,0:T(8,128)(2,1)S(1)}, u32[]{:S(2)}, u32[]{:S(2)}) %collective-permute-start.4) | collective-permute-done | bytes 131104 | tf_op jit(solution)/shard_map/ppermute | solution.py:403
  162.9 2.1 %collective-permute-start.9 = (bf16[128,512]{1,0:T(8,128)(2,1)S(1)}, bf16[128,512]{1,0:T(8,128)(2,1)S(1)}, u32[]{:S(2)}, u32[]{:S(2)}) collective-permute-start(bf16[128,512]{1,0:T(8,128)(2,1)S(1)} %get-tuple-element.60), channel_id=1, source_target_pairs={{0,24},{1,25},{2,26},{3,27},{4,28},{5,29},{6,30},{7,31},{8,0},{9,1... | collective-permute-start | bytes 393224 | tf_op jit(solution)/shard_map/ppermute | solution.py:403
  165.0 2.3 %collective-permute-done.5 = bf16[128,512]{1,0:T(8,128)(2,1)S(1)} collective-permute-done((bf16[128,512]{1,0:T(8,128)(2,1)S(1)}, bf16[128,512]{1,0:T(8,128)(2,1)S(1)}, u32[]{:S(2)}, u32[]{:S(2)}) %collective-permute-start.5) | collective-permute-done | bytes 131104 | tf_op jit(solution)/shard_map/ppermute | solution.py:403
  167.5 0.9 collective-permute-start.11
  168.5 1.4 collective-permute-start.10
  169.9 5.0 %shard_map.78 = bf16[16,64,512]{2,1,0:T(8,128)(2,1)} custom-call(s32[2,32]{1,0:T(2,128)S(1)} %get-tuple-element.62.send_ref, f32[16,64,512]{2,1,0:T(8,128)S(1)} %bitcast.64, bf16[32,2,64,512]{3,2,1,0:T(8,128)(2,1)} %all-to-all-done.1.returned_ref), custom_call_target="tpu_custom_call" | custom-call | tf_op jit(solution)/shard_map/pallas_call | solution.py:358
  175.0 1.6 collective-permute-start.12
  176.6 1.8 collective-permute-start.13
  178.4 1.7 collective-permute-done.12
  180.1 1.8 collective-permute-done.13
  182.0 3.7 %collective-permute-start.14 = (bf16[2,128,512]{2,1,0:T(8,128)(2,1)S(1)}, bf16[2,128,512]{2,1,0:T(8,128)(2,1)S(1)}, u32[]{:S(2)}, u32[]{:S(2)}) collective-permute-start(bf16[2,128,512]{2,1,0:T(8,128)(2,1)S(1)} %pad_maximum_fusion.2), channel_id=1, source_target_pairs={{0,1},{1,0},{2,3},{3,2},{4,5},{5,4},{6,7},{7,6},{8,9},{9,8},{10,11... | collective-permute-start | bytes 786440 | tf_op jit(solution)/shard_map/ppermute | solution.py:490
  185.7 1.2 collective-permute-done.14
  186.9 1.1 pad_maximum_fusion.1
  (62 shorter events, 2.2 us)
Async XLA Ops:
  0.6 15.5 %copy-start = (s32[512,64]{0,1:T(8,128)S(1)}, s32[512,64]{0,1:T(8,128)}, u32[]{:S(2)}) copy-start(s32[512,64]{0,1:T(8,128)} %param.9) | copy-start | bytes 393220
  6.3 11.9 %copy-start.2 = (bf16[4,512,512]{2,1,0:T(8,128)(2,1)S(1)}, bf16[4,512,512]{2,1,0:T(8,128)(2,1)}, u32[]{:S(2)}) copy-start(bf16[4,512,512]{2,1,0:T(8,128)(2,1)} %param.6) | copy-start | bytes 6291460
  6.3 59.0 %all-to-all-start = ((bf16[32,2,64,512]{3,2,1,0:T(8,128)(2,1)}), bf16[32,2,64,512]{3,2,1,0:T(8,128)(2,1)}, u32[]{:S(2)}, u32[]{:S(2)}) async-start(bf16[32,2,64,512]{3,2,1,0:T(8,128)(2,1)} %bitcast.65), calls=%async_computation | async-start | bytes 8388608 | tf_op jit(solution)/shard_map/all_to_all | solution.py:442
  18.2 2.5 %copy-start.1 = (bf16[1,1024,512]{2,1,0:T(8,128)(2,1)S(1)}, bf16[1,1024,512]{2,1,0:T(8,128)(2,1)}, u32[]{:S(2)}) copy-start(bf16[1,1024,512]{2,1,0:T(8,128)(2,1)} %param.5) | copy-start | bytes 3145732
  24.0 1.7 copy-start.8
  102.8 64.6 %all-to-all-start.1 = ((bf16[32,2,64,512]{3,2,1,0:T(8,128)(2,1)}), bf16[32,2,64,512]{3,2,1,0:T(8,128)(2,1)}, u32[]{:S(2)}, u32[]{:S(2)}) async-start(bf16[32,2,64,512]{3,2,1,0:T(8,128)(2,1)} %get-tuple-element.35), calls=%async_computation.1 | async-start | bytes 8388608 | tf_op jit(solution)/shard_map/all_to_all | solution.py:459
  111.0 15.0 %copy-start.7 = (bf16[1024,512]{1,0:T(8,128)(2,1)S(1)}, bf16[1024,512]{1,0:T(8,128)(2,1)}, u32[]{:S(2)}) copy-start(bf16[1024,512]{1,0:T(8,128)(2,1)} %get-tuple-element.29.gq_ref) | copy-start | bytes 3145732
  125.6 1.2 copy-start.6
  125.6 3.9 %collective-permute-start = (bf16[2,512,512]{2,1,0:T(8,128)(2,1)}, bf16[2,512,512]{2,1,0:T(8,128)(2,1)S(1)}, u32[]{:S(2)}, u32[]{:S(2)}) collective-permute-start(bf16[2,512,512]{2,1,0:T(8,128)(2,1)} %get-tuple-element.32), channel_id=1, source_target_pairs={{0,1},{1,0},{2,3},{3,2},{4,5},{5,4},{6,7},{7,6},{8,9},{9,8},{10,11... | collective-permute-start | bytes 3145736 | tf_op jit(solution)/shard_map/ppermute | solution.py:376
  126.9 1.6 copy-start.3
  126.9 1.9 copy-start.5
  128.7 1.6 copy-start.4
  130.3 6.2 %copy-start.9 = (bf16[1024,512]{1,0:T(8,128)(2,1)S(1)}, bf16[1024,512]{1,0:T(8,128)(2,1)}, u32[]{:S(2)}) copy-start(bf16[1024,512]{1,0:T(8,128)(2,1)} %get-tuple-element.30.att_ref) | copy-start | bytes 3145732
  130.8 10.3 %collective-permute-start.1 = (bf16[2,128,512]{2,1,0:T(8,128)(2,1)S(1)}, bf16[2,128,512]{2,1,0:T(8,128)(2,1)S(1)}, u32[]{:S(2)}, u32[]{:S(2)}) collective-permute-start(bf16[2,128,512]{2,1,0:T(8,128)(2,1)S(1)} %get-tuple-element.49), channel_id=1, source_target_pairs={{0,32},{32,64},{64,96},{96,0},{1,33},{33,65},{65,97},{97,1},{2,34}... | collective-permute-start | bytes 786440 | tf_op jit(solution)/shard_map/ppermute | solution.py:384
  132.5 15.0 %collective-permute-start.2 = (bf16[2,128,512]{2,1,0:T(8,128)(2,1)S(1)}, bf16[2,128,512]{2,1,0:T(8,128)(2,1)S(1)}, u32[]{:S(2)}, u32[]{:S(2)}) collective-permute-start(bf16[2,128,512]{2,1,0:T(8,128)(2,1)S(1)} %get-tuple-element.51), channel_id=1, source_target_pairs={{0,64},{32,96},{64,0},{96,32},{1,65},{33,97},{65,1},{97,33},{2,66}... | collective-permute-start | bytes 786440 | tf_op jit(solution)/shard_map/ppermute | solution.py:384
  135.8 11.7 %collective-permute-start.3 = (bf16[2,128,512]{2,1,0:T(8,128)(2,1)S(1)}, bf16[2,128,512]{2,1,0:T(8,128)(2,1)S(1)}, u32[]{:S(2)}, u32[]{:S(2)}) collective-permute-start(bf16[2,128,512]{2,1,0:T(8,128)(2,1)S(1)} %get-tuple-element.50), channel_id=1, source_target_pairs={{0,96},{32,0},{64,32},{96,64},{1,97},{33,1},{65,33},{97,65},{2,98}... | collective-permute-start | bytes 786440 | tf_op jit(solution)/shard_map/ppermute | solution.py:384
  147.7 15.2 %collective-permute-start.4 = (bf16[128,512]{1,0:T(8,128)(2,1)S(1)}, bf16[128,512]{1,0:T(8,128)(2,1)S(1)}, u32[]{:S(2)}, u32[]{:S(2)}) collective-permute-start(bf16[128,512]{1,0:T(8,128)(2,1)S(1)} %get-tuple-element.61), channel_id=1, source_target_pairs={{0,2},{1,3},{2,4},{3,5},{4,6},{5,7},{6,0},{7,1},{8,10},{9,11},{10,... | collective-permute-start | bytes 393224 | tf_op jit(solution)/shard_map/ppermute | solution.py:403
  149.2 18.1 %collective-permute-start.5 = (bf16[128,512]{1,0:T(8,128)(2,1)S(1)}, bf16[128,512]{1,0:T(8,128)(2,1)S(1)}, u32[]{:S(2)}, u32[]{:S(2)}) collective-permute-start(bf16[128,512]{1,0:T(8,128)(2,1)S(1)} %get-tuple-element.61), channel_id=1, source_target_pairs={{0,4},{1,5},{2,6},{3,7},{4,0},{5,1},{6,2},{7,3},{8,12},{9,13},{10,... | collective-permute-start | bytes 393224 | tf_op jit(solution)/shard_map/ppermute | solution.py:403
  151.7 15.7 %collective-permute-start.6 = (bf16[128,512]{1,0:T(8,128)(2,1)S(1)}, bf16[128,512]{1,0:T(8,128)(2,1)S(1)}, u32[]{:S(2)}, u32[]{:S(2)}) collective-permute-start(bf16[128,512]{1,0:T(8,128)(2,1)S(1)} %get-tuple-element.61), channel_id=1, source_target_pairs={{0,6},{1,7},{2,0},{3,1},{4,2},{5,3},{6,4},{7,5},{8,14},{9,15},{10,... | collective-permute-start | bytes 393224 | tf_op jit(solution)/shard_map/ppermute | solution.py:403
  152.8 14.5 %collective-permute-start.7 = (bf16[128,512]{1,0:T(8,128)(2,1)S(1)}, bf16[128,512]{1,0:T(8,128)(2,1)S(1)}, u32[]{:S(2)}, u32[]{:S(2)}) collective-permute-start(bf16[128,512]{1,0:T(8,128)(2,1)S(1)} %get-tuple-element.60), channel_id=1, source_target_pairs={{0,8},{1,9},{2,10},{3,11},{4,12},{5,13},{6,14},{7,15},{8,16},{9,17... | collective-permute-start | bytes 393224 | tf_op jit(solution)/shard_map/ppermute | solution.py:403
  153.9 13.4 %collective-permute-start.8 = (bf16[128,512]{1,0:T(8,128)(2,1)S(1)}, bf16[128,512]{1,0:T(8,128)(2,1)S(1)}, u32[]{:S(2)}, u32[]{:S(2)}) collective-permute-start(bf16[128,512]{1,0:T(8,128)(2,1)S(1)} %get-tuple-element.60), channel_id=1, source_target_pairs={{0,16},{1,17},{2,18},{3,19},{4,20},{5,21},{6,22},{7,23},{8,24},{9,... | collective-permute-start | bytes 393224 | tf_op jit(solution)/shard_map/ppermute | solution.py:403
  162.9 4.4 %collective-permute-start.9 = (bf16[128,512]{1,0:T(8,128)(2,1)S(1)}, bf16[128,512]{1,0:T(8,128)(2,1)S(1)}, u32[]{:S(2)}, u32[]{:S(2)}) collective-permute-start(bf16[128,512]{1,0:T(8,128)(2,1)S(1)} %get-tuple-element.60), channel_id=1, source_target_pairs={{0,24},{1,25},{2,26},{3,27},{4,28},{5,29},{6,30},{7,31},{8,0},{9,1... | collective-permute-start | bytes 393224 | tf_op jit(solution)/shard_map/ppermute | solution.py:403
  167.5 7.3 %collective-permute-start.11 = (bf16[128,512]{1,0:T(8,128)(2,1)S(1)}, bf16[128,512]{1,0:T(8,128)(2,1)S(1)}, u32[]{:S(2)}, u32[]{:S(2)}) collective-permute-start(bf16[128,512]{1,0:T(8,128)(2,1)S(1)} %get-tuple-element.58), channel_id=1, source_target_pairs={{0,2},{1,3},{2,0},{3,1},{4,6},{5,7},{6,4},{7,5},{8,10},{9,11},{10,... | collective-permute-start | bytes 393224 | tf_op jit(solution)/shard_map/ppermute | solution.py:413
  168.5 6.4 %collective-permute-start.10 = (bf16[128,512]{1,0:T(8,128)(2,1)S(1)}, bf16[128,512]{1,0:T(8,128)(2,1)S(1)}, u32[]{:S(2)}, u32[]{:S(2)}) collective-permute-start(bf16[128,512]{1,0:T(8,128)(2,1)S(1)} %get-tuple-element.59), channel_id=1, source_target_pairs={{0,8},{1,9},{2,10},{3,11},{4,12},{5,13},{6,14},{7,15},{8,0},{9,1},... | collective-permute-start | bytes 393224 | tf_op jit(solution)/shard_map/ppermute | solution.py:413
  175.0 5.1 %collective-permute-start.12 = (bf16[128,512]{1,0:T(8,128)(2,1)S(1)}, bf16[128,512]{1,0:T(8,128)(2,1)S(1)}, u32[]{:S(2)}, u32[]{:S(2)}) collective-permute-start(bf16[128,512]{1,0:T(8,128)(2,1)S(1)} %add_convert_fusion.4), channel_id=1, source_target_pairs={{0,24},{1,25},{2,26},{3,27},{4,28},{5,29},{6,30},{7,31},{8,16},{9,... | collective-permute-start | bytes 393224 | tf_op jit(solution)/shard_map/ppermute | solution.py:413
  176.6 5.3 %collective-permute-start.13 = (bf16[128,512]{1,0:T(8,128)(2,1)S(1)}, bf16[128,512]{1,0:T(8,128)(2,1)S(1)}, u32[]{:S(2)}, u32[]{:S(2)}) collective-permute-start(bf16[128,512]{1,0:T(8,128)(2,1)S(1)} %add_convert_fusion.2), channel_id=1, source_target_pairs={{0,6},{1,7},{2,4},{3,5},{4,2},{5,3},{6,0},{7,1},{8,14},{9,15},{10,... | collective-permute-start | bytes 393224 | tf_op jit(solution)/shard_map/ppermute | solution.py:413
  182.0 4.9 %collective-permute-start.14 = (bf16[2,128,512]{2,1,0:T(8,128)(2,1)S(1)}, bf16[2,128,512]{2,1,0:T(8,128)(2,1)S(1)}, u32[]{:S(2)}, u32[]{:S(2)}) collective-permute-start(bf16[2,128,512]{2,1,0:T(8,128)(2,1)S(1)} %pad_maximum_fusion.2), channel_id=1, source_target_pairs={{0,1},{1,0},{2,3},{3,2},{4,5},{5,4},{6,7},{7,6},{8,9},{9,8},{10,11... | collective-permute-start | bytes 786440 | tf_op jit(solution)/shard_map/ppermute | solution.py:490

commit v2 on v0

--- a/solution.py
+++ b/solution.py
@@ -141,8 +141,16 @@
         def second_half(at, cols, ids, ends, qbd, ubd, k_all, v_all, scores, dprob):
             scores = jnp.concatenate(
                 [
-                    jnp.where(place < ends[n], scores[n * BS : (n + 1) * BS], -1e30)
+                    piece
                     for n in range(NNB)
+                    for piece in (
+                        scores[n * BS : n * BS + BS // 2],
+                        jnp.where(
+                            place[BS // 2 :] < ends[n],
+                            scores[n * BS + BS // 2 : (n + 1) * BS],
+                            -1e30,
+                        ),
+                    )
                 ],
                 axis=0,
             )
@@ -354,7 +362,7 @@
 def combine_call(send, base, returned):
     blocks, _, dim = base.shape
     parts = returned.shape[0]
-    per = 8
+    per = 16
     return pl.pallas_call(
         functools.partial(combine_kernel, per),
         grid_spec=pltpu.PrefetchScalarGridSpec(

time: 189 us -> 188 us (level)
  transfers between devices with their start and end apart: 17 -> 17, of which waited for: 8 -> 9; matrix products, arithmetic and copies ran while one was open for 9% -> 9% of each run, Pallas kernels for 10% -> 10%
where the time goes in v2:
time: 188 us
  waiting for transfers between devices  61 us (32%)
  Pallas kernels  56 us (30%)
  starting transfers between devices  44 us (23%)
  matrix products  10.7 us (6%)
  local copies, waits for them, and re-layouts  9.47 us (5%)
  other arithmetic  5.6 us (3%)
    all_to_all x1, waiting for transfers between devices, local(): lax.all_to_all(inputs_now.reshape(blocks, BS, dim)[send.T.reshape(-1)].re...  38 us
    pallas_call x1, Pallas kernels, layer_call(): pl.pallas_call(functools.partial(layer_kernel, scaling), grid_spec=pltpu....  37.1 us
    pallas_call x1, Pallas kernels, weights_call(): pl.pallas_call(functools.partial(weights_kernel, steps_far), grid_spec=pl...  14.6 us
    ppermute x6, starting transfers between devices, ring_parts(): return [lax.ppermute(value, 'verts', move) for move in moves]  10.8 us
    ppermute x3, waiting for transfers between devices, over_cores_and_planes(): lax.ppermute(there.astype(jnp.bfloat16), 'dp', move).astype(jnp.float32)  9.25 us
    all_to_all x1, starting transfers between devices, local(): lax.all_to_all(inputs_now.reshape(blocks, BS, dim)[send.T.reshape(-1)].re...  8.78 us
    ppermute x6, waiting for transfers between devices, ring_parts(): return [lax.ppermute(value, 'verts', move) for move in moves]  8.77 us
    all_to_all x1, starting transfers between devices, local(): lax.all_to_all(back, 'verts', split_axis=0, concat_axis=0, tiled=True)  7.99 us
  transfers between devices with their start and end apart: 17, of which 9 were waited for; matrix products, arithmetic and copies ran while one was open for 9% of the time, Pallas kernels for 10%

profile of v2, /device:TPU:1, one launch (start us, length us, event | category | flops | bytes accessed | tf_op | source)
XLA Modules:
  0.0 187.8 jit_solution(3207807965097392092)
XLA Ops:
  0.8 0.8 select_reduce_fusion.3
  2.3 4.0 %gather_fusion = bf16[64,64,512]{2,1,0:T(8,128)(2,1)} fusion(bf16[16,64,512]{2,1,0:T(8,128)(2,1)} %bitcast.66, s32[1024]{0:T(1024)S(1)} %pad_clamp_fusion.1), kind=kCustom, calls=%fused_computation | custom fusion | bytes 8388864 | tf_op jit(solution)/shard_map/gather | solution.py:451
  6.3 8.8 %all-to-all-start = ((bf16[32,2,64,512]{3,2,1,0:T(8,128)(2,1)}), bf16[32,2,64,512]{3,2,1,0:T(8,128)(2,1)}, u32[]{:S(2)}, u32[]{:S(2)}) async-start(bf16[32,2,64,512]{3,2,1,0:T(8,128)(2,1)} %bitcast.65), calls=%async_computation | async-start | bytes 8388608 | tf_op jit(solution)/shard_map/all_to_all | solution.py:450
  15.1 0.8 constant_dynamic-slice_fusion
  16.1 1.8 gather_fusion.1
  18.3 1.1 pad_maximum_fusion.wkv_hbm
  19.4 0.5 compare_select_fusion.5.entries
  19.9 0.7 compare_convert_fusion.diag_ref
  20.6 1.7 convolution_convert_fusion.4
  22.3 1.7 convolution_convert_fusion.3
  24.0 1.7 convolution_convert_fusion.2.q_hbm
  25.7 1.7 convolution_convert_fusion.1.u_hbm
  27.4 38.0 %all-to-all-done.far_hbm.far_ref = bf16[32,2,64,512]{3,2,1,0:T(8,128)(2,1)} async-done(((bf16[32,2,64,512]{3,2,1,0:T(8,128)(2,1)}), bf16[32,2,64,512]{3,2,1,0:T(8,128)(2,1)}, u32[]{:S(2)}, u32[]{:S(2)}) %all-to-all-start) | async-done | bytes 4194336 | tf_op jit(solution)/shard_map/all_to_all | solution.py:450
  65.3 37.1 %shard_map.76 = (bf16[1024,512]{1,0:T(8,128)(2,1)}, bf16[1024,512]{1,0:T(8,128)(2,1)}, bf16[64,64,512]{2,1,0:T(8,128)(2,1)}, bf16[64,64,512]{2,1,0:T(8,128)(2,1)...) custom-call(s32[128]{0:T(128)} %compare_select_fusion.5.entries, ...), custom_call_target="tpu_custom_call" | custom-call | tf_op jit(solution)/shard_map/pallas_call | solution.py:235
  102.4 8.0 %all-to-all-start.1 = ((bf16[32,2,64,512]{3,2,1,0:T(8,128)(2,1)}), bf16[32,2,64,512]{3,2,1,0:T(8,128)(2,1)}, u32[]{:S(2)}, u32[]{:S(2)}) async-start(bf16[32,2,64,512]{3,2,1,0:T(8,128)(2,1)} %get-tuple-element.35), calls=%async_computation.1 | async-start | bytes 8388608 | tf_op jit(solution)/shard_map/all_to_all | solution.py:467
  110.5 14.6 %shard_map.77 = (f32[2,512,512]{2,1,0:T(8,128)}, bf16[2,512,512]{2,1,0:T(8,128)(2,1)}) custom-call(s32[1]{0:T(128)} %bitcast.core, bf16[32,2,64,512]{3,2,1,0:T(8,128)(2,1)} %all-to-all-done.far_hbm.far_ref, bf16[64,64,512]{2,1,0:T(8,128)(2,1)} %get-tuple-element.25.gk_ref, bf16[64,64,512]{2,1,0:T(8,128)(2,1)} %get-tuple-element.26.gv_ref, ...), custom_call_target="tpu_custom_call" | custom-call | flops 11000000512 | bytes 20000000 | tf_op jit(solution)/shard_map/pallas_call | solution.py:318
  125.1 0.6 collective-permute-start
  125.7 0.7 fusion.2
  126.5 0.7 fusion.22
  127.2 0.8 copy-done.3
  128.0 0.3 copy-done.5
  128.3 0.8 add_add_fusion
  129.1 0.8 copy-done.4
  129.9 0.4 convert_add_fusion
  130.4 1.7 collective-permute-start.1
  132.1 3.3 %collective-permute-start.2 = (bf16[2,128,512]{2,1,0:T(8,128)(2,1)S(1)}, bf16[2,128,512]{2,1,0:T(8,128)(2,1)S(1)}, u32[]{:S(2)}, u32[]{:S(2)}) collective-permute-start(bf16[2,128,512]{2,1,0:T(8,128)(2,1)S(1)} %get-tuple-element.51), channel_id=1, source_target_pairs={{0,64},{32,96},{64,0},{96,32},{1,65},{33,97},{65,1},{97,33},{2,66}... | collective-permute-start | bytes 786440 | tf_op jit(solution)/shard_map/ppermute | solution.py:392
  135.4 0.7 collective-permute-start.3
  136.1 1.7 convolution_convert_fusion
  137.8 2.8 %collective-permute-done.1 = bf16[2,128,512]{2,1,0:T(8,128)(2,1)S(1)} collective-permute-done((bf16[2,128,512]{2,1,0:T(8,128)(2,1)S(1)}, bf16[2,128,512]{2,1,0:T(8,128)(2,1)S(1)}, u32[]{:S(2)}, u32[]{:S(2)}) %collective-permute-start.1) | collective-permute-done | bytes 262176 | tf_op jit(solution)/shard_map/ppermute | solution.py:392
  140.6 6.5 %collective-permute-done.2 = bf16[2,128,512]{2,1,0:T(8,128)(2,1)S(1)} collective-permute-done((bf16[2,128,512]{2,1,0:T(8,128)(2,1)S(1)}, bf16[2,128,512]{2,1,0:T(8,128)(2,1)S(1)}, u32[]{:S(2)}, u32[]{:S(2)}) %collective-permute-start.2) | collective-permute-done | bytes 262176 | tf_op jit(solution)/shard_map/ppermute | solution.py:392
  147.2 1.5 collective-permute-start.4
  148.7 2.4 %collective-permute-start.5 = (bf16[128,512]{1,0:T(8,128)(2,1)S(1)}, bf16[128,512]{1,0:T(8,128)(2,1)S(1)}, u32[]{:S(2)}, u32[]{:S(2)}) collective-permute-start(bf16[128,512]{1,0:T(8,128)(2,1)S(1)} %get-tuple-element.61), channel_id=1, source_target_pairs={{0,4},{1,5},{2,6},{3,7},{4,0},{5,1},{6,2},{7,3},{8,12},{9,13},{10,... | collective-permute-start | bytes 393224 | tf_op jit(solution)/shard_map/ppermute | solution.py:411
  151.1 1.2 collective-permute-start.6
  152.3 1.1 collective-permute-start.7
  153.4 2.6 %collective-permute-start.8 = (bf16[128,512]{1,0:T(8,128)(2,1)S(1)}, bf16[128,512]{1,0:T(8,128)(2,1)S(1)}, u32[]{:S(2)}, u32[]{:S(2)}) collective-permute-start(bf16[128,512]{1,0:T(8,128)(2,1)S(1)} %get-tuple-element.60), channel_id=1, source_target_pairs={{0,16},{1,17},{2,18},{3,19},{4,20},{5,21},{6,22},{7,23},{8,24},{9,... | collective-permute-start | bytes 393224 | tf_op jit(solution)/shard_map/ppermute | solution.py:411
  156.0 6.4 %collective-permute-done.4 = bf16[128,512]{1,0:T(8,128)(2,1)S(1)} collective-permute-done((bf16[128,512]{1,0:T(8,128)(2,1)S(1)}, bf16[128,512]{1,0:T(8,128)(2,1)S(1)}, u32[]{:S(2)}, u32[]{:S(2)}) %collective-permute-start.4) | collective-permute-done | bytes 131104 | tf_op jit(solution)/shard_map/ppermute | solution.py:411
  162.4 2.1 %collective-permute-start.9 = (bf16[128,512]{1,0:T(8,128)(2,1)S(1)}, bf16[128,512]{1,0:T(8,128)(2,1)S(1)}, u32[]{:S(2)}, u32[]{:S(2)}) collective-permute-start(bf16[128,512]{1,0:T(8,128)(2,1)S(1)} %get-tuple-element.60), channel_id=1, source_target_pairs={{0,24},{1,25},{2,26},{3,27},{4,28},{5,29},{6,30},{7,31},{8,0},{9,1... | collective-permute-start | bytes 393224 | tf_op jit(solution)/shard_map/ppermute | solution.py:411
  164.4 2.2 %collective-permute-done.5 = bf16[128,512]{1,0:T(8,128)(2,1)S(1)} collective-permute-done((bf16[128,512]{1,0:T(8,128)(2,1)S(1)}, bf16[128,512]{1,0:T(8,128)(2,1)S(1)}, u32[]{:S(2)}, u32[]{:S(2)}) %collective-permute-start.5) | collective-permute-done | bytes 131104 | tf_op jit(solution)/shard_map/ppermute | solution.py:411
  167.0 1.0 collective-permute-start.11
  168.0 1.1 collective-permute-start.10
  169.1 4.3 %shard_map.78 = bf16[16,64,512]{2,1,0:T(8,128)(2,1)} custom-call(s32[2,32]{1,0:T(2,128)S(1)} %get-tuple-element.62.send_ref, f32[16,64,512]{2,1,0:T(8,128)S(1)} %bitcast.64, bf16[32,2,64,512]{3,2,1,0:T(8,128)(2,1)} %all-to-all-done.1.returned_ref), custom_call_target="tpu_custom_call" | custom-call | tf_op jit(solution)/shard_map/pallas_call | solution.py:366
  173.5 1.8 collective-permute-start.12
  175.3 1.8 collective-permute-start.13
  177.1 1.5 collective-permute-done.12
  178.6 2.0 %collective-permute-done.13 = bf16[128,512]{1,0:T(8,128)(2,1)S(1)} collective-permute-done((bf16[128,512]{1,0:T(8,128)(2,1)S(1)}, bf16[128,512]{1,0:T(8,128)(2,1)S(1)}, u32[]{:S(2)}, u32[]{:S(2)}) %collective-permute-start.13) | collective-permute-done | bytes 131104 | tf_op jit(solution)/shard_map/ppermute | solution.py:421
  180.7 4.3 %collective-permute-start.14 = (f32[2,128,512]{2,1,0:T(8,128)S(1)}, f32[2,128,512]{2,1,0:T(8,128)S(1)}, u32[]{:S(2)}, u32[]{:S(2)}) collective-permute-start(f32[2,128,512]{2,1,0:T(8,128)S(1)} %pad_maximum_fusion.2), channel_id=1, source_target_pairs={{0,1},{1,0},{2,3},{3,2},{4,5},{5,4},{6,7},{7,6},{8,9},{9,8},{10,11... | collective-permute-start | bytes 1572872 | tf_op jit(solution)/shard_map/ppermute | solution.py:498
  185.0 1.5 collective-permute-done.14
  186.7 1.1 pad_maximum_fusion.1
  (62 shorter events, 2.3 us)
Async XLA Ops:
  0.6 15.5 %copy-start = (s32[512,64]{0,1:T(8,128)S(1)}, s32[512,64]{0,1:T(8,128)}, u32[]{:S(2)}) copy-start(s32[512,64]{0,1:T(8,128)} %param.9) | copy-start | bytes 393220
  6.3 11.9 %copy-start.2 = (bf16[4,512,512]{2,1,0:T(8,128)(2,1)S(1)}, bf16[4,512,512]{2,1,0:T(8,128)(2,1)}, u32[]{:S(2)}) copy-start(bf16[4,512,512]{2,1,0:T(8,128)(2,1)} %param.6) | copy-start | bytes 6291460
  6.3 59.0 %all-to-all-start = ((bf16[32,2,64,512]{3,2,1,0:T(8,128)(2,1)}), bf16[32,2,64,512]{3,2,1,0:T(8,128)(2,1)}, u32[]{:S(2)}, u32[]{:S(2)}) async-start(bf16[32,2,64,512]{3,2,1,0:T(8,128)(2,1)} %bitcast.65), calls=%async_computation | async-start | bytes 8388608 | tf_op jit(solution)/shard_map/all_to_all | solution.py:450
  18.2 2.5 %copy-start.1 = (bf16[1,1024,512]{2,1,0:T(8,128)(2,1)S(1)}, bf16[1,1024,512]{2,1,0:T(8,128)(2,1)}, u32[]{:S(2)}) copy-start(bf16[1,1024,512]{2,1,0:T(8,128)(2,1)} %param.5) | copy-start | bytes 3145732
  24.0 1.7 copy-start.8
  102.4 64.4 %all-to-all-start.1 = ((bf16[32,2,64,512]{3,2,1,0:T(8,128)(2,1)}), bf16[32,2,64,512]{3,2,1,0:T(8,128)(2,1)}, u32[]{:S(2)}, u32[]{:S(2)}) async-start(bf16[32,2,64,512]{3,2,1,0:T(8,128)(2,1)} %get-tuple-element.35), calls=%async_computation.1 | async-start | bytes 8388608 | tf_op jit(solution)/shard_map/all_to_all | solution.py:467
  110.5 15.2 %copy-start.7 = (bf16[1024,512]{1,0:T(8,128)(2,1)S(1)}, bf16[1024,512]{1,0:T(8,128)(2,1)}, u32[]{:S(2)}) copy-start(bf16[1024,512]{1,0:T(8,128)(2,1)} %get-tuple-element.29.gq_ref) | copy-start | bytes 3145732
  125.1 1.3 copy-start.6
  125.1 4.0 %collective-permute-start = (bf16[2,512,512]{2,1,0:T(8,128)(2,1)}, bf16[2,512,512]{2,1,0:T(8,128)(2,1)S(1)}, u32[]{:S(2)}, u32[]{:S(2)}) collective-permute-start(bf16[2,512,512]{2,1,0:T(8,128)(2,1)} %get-tuple-element.32), channel_id=1, source_target_pairs={{0,1},{1,0},{2,3},{3,2},{4,5},{5,4},{6,7},{7,6},{8,9},{9,8},{10,11... | collective-permute-start | bytes 3145736 | tf_op jit(solution)/shard_map/ppermute | solution.py:384
  126.4 1.6 copy-start.3
  126.5 1.8 copy-start.5
  128.3 1.6 copy-start.4
  129.9 6.2 %copy-start.9 = (bf16[1024,512]{1,0:T(8,128)(2,1)S(1)}, bf16[1024,512]{1,0:T(8,128)(2,1)}, u32[]{:S(2)}) copy-start(bf16[1024,512]{1,0:T(8,128)(2,1)} %get-tuple-element.30.att_ref) | copy-start | bytes 3145732
  130.4 10.2 %collective-permute-start.1 = (bf16[2,128,512]{2,1,0:T(8,128)(2,1)S(1)}, bf16[2,128,512]{2,1,0:T(8,128)(2,1)S(1)}, u32[]{:S(2)}, u32[]{:S(2)}) collective-permute-start(bf16[2,128,512]{2,1,0:T(8,128)(2,1)S(1)} %get-tuple-element.49), channel_id=1, source_target_pairs={{0,32},{32,64},{64,96},{96,0},{1,33},{33,65},{65,97},{97,1},{2,34}... | collective-permute-start | bytes 786440 | tf_op jit(solution)/shard_map/ppermute | solution.py:392
  132.1 15.0 %collective-permute-start.2 = (bf16[2,128,512]{2,1,0:T(8,128)(2,1)S(1)}, bf16[2,128,512]{2,1,0:T(8,128)(2,1)S(1)}, u32[]{:S(2)}, u32[]{:S(2)}) collective-permute-start(bf16[2,128,512]{2,1,0:T(8,128)(2,1)S(1)} %get-tuple-element.51), channel_id=1, source_target_pairs={{0,64},{32,96},{64,0},{96,32},{1,65},{33,97},{65,1},{97,33},{2,66}... | collective-permute-start | bytes 786440 | tf_op jit(solution)/shard_map/ppermute | solution.py:392
  135.4 11.7 %collective-permute-start.3 = (bf16[2,128,512]{2,1,0:T(8,128)(2,1)S(1)}, bf16[2,128,512]{2,1,0:T(8,128)(2,1)S(1)}, u32[]{:S(2)}, u32[]{:S(2)}) collective-permute-start(bf16[2,128,512]{2,1,0:T(8,128)(2,1)S(1)} %get-tuple-element.50), channel_id=1, source_target_pairs={{0,96},{32,0},{64,32},{96,64},{1,97},{33,1},{65,33},{97,65},{2,98}... | collective-permute-start | bytes 786440 | tf_op jit(solution)/shard_map/ppermute | solution.py:392
  147.2 15.2 %collective-permute-start.4 = (bf16[128,512]{1,0:T(8,128)(2,1)S(1)}, bf16[128,512]{1,0:T(8,128)(2,1)S(1)}, u32[]{:S(2)}, u32[]{:S(2)}) collective-permute-start(bf16[128,512]{1,0:T(8,128)(2,1)S(1)} %get-tuple-element.61), channel_id=1, source_target_pairs={{0,2},{1,3},{2,4},{3,5},{4,6},{5,7},{6,0},{7,1},{8,10},{9,11},{10,... | collective-permute-start | bytes 393224 | tf_op jit(solution)/shard_map/ppermute | solution.py:411
  148.7 17.9 %collective-permute-start.5 = (bf16[128,512]{1,0:T(8,128)(2,1)S(1)}, bf16[128,512]{1,0:T(8,128)(2,1)S(1)}, u32[]{:S(2)}, u32[]{:S(2)}) collective-permute-start(bf16[128,512]{1,0:T(8,128)(2,1)S(1)} %get-tuple-element.61), channel_id=1, source_target_pairs={{0,4},{1,5},{2,6},{3,7},{4,0},{5,1},{6,2},{7,3},{8,12},{9,13},{10,... | collective-permute-start | bytes 393224 | tf_op jit(solution)/shard_map/ppermute | solution.py:411
  151.1 15.5 %collective-permute-start.6 = (bf16[128,512]{1,0:T(8,128)(2,1)S(1)}, bf16[128,512]{1,0:T(8,128)(2,1)S(1)}, u32[]{:S(2)}, u32[]{:S(2)}) collective-permute-start(bf16[128,512]{1,0:T(8,128)(2,1)S(1)} %get-tuple-element.61), channel_id=1, source_target_pairs={{0,6},{1,7},{2,0},{3,1},{4,2},{5,3},{6,4},{7,5},{8,14},{9,15},{10,... | collective-permute-start | bytes 393224 | tf_op jit(solution)/shard_map/ppermute | solution.py:411
  152.3 14.4 %collective-permute-start.7 = (bf16[128,512]{1,0:T(8,128)(2,1)S(1)}, bf16[128,512]{1,0:T(8,128)(2,1)S(1)}, u32[]{:S(2)}, u32[]{:S(2)}) collective-permute-start(bf16[128,512]{1,0:T(8,128)(2,1)S(1)} %get-tuple-element.60), channel_id=1, source_target_pairs={{0,8},{1,9},{2,10},{3,11},{4,12},{5,13},{6,14},{7,15},{8,16},{9,17... | collective-permute-start | bytes 393224 | tf_op jit(solution)/shard_map/ppermute | solution.py:411
  153.4 13.2 %collective-permute-start.8 = (bf16[128,512]{1,0:T(8,128)(2,1)S(1)}, bf16[128,512]{1,0:T(8,128)(2,1)S(1)}, u32[]{:S(2)}, u32[]{:S(2)}) collective-permute-start(bf16[128,512]{1,0:T(8,128)(2,1)S(1)} %get-tuple-element.60), channel_id=1, source_target_pairs={{0,16},{1,17},{2,18},{3,19},{4,20},{5,21},{6,22},{7,23},{8,24},{9,... | collective-permute-start | bytes 393224 | tf_op jit(solution)/shard_map/ppermute | solution.py:411
  162.4 4.4 %collective-permute-start.9 = (bf16[128,512]{1,0:T(8,128)(2,1)S(1)}, bf16[128,512]{1,0:T(8,128)(2,1)S(1)}, u32[]{:S(2)}, u32[]{:S(2)}) collective-permute-start(bf16[128,512]{1,0:T(8,128)(2,1)S(1)} %get-tuple-element.60), channel_id=1, source_target_pairs={{0,24},{1,25},{2,26},{3,27},{4,28},{5,29},{6,30},{7,31},{8,0},{9,1... | collective-permute-start | bytes 393224 | tf_op jit(solution)/shard_map/ppermute | solution.py:411
  167.0 6.4 %collective-permute-start.11 = (bf16[128,512]{1,0:T(8,128)(2,1)S(1)}, bf16[128,512]{1,0:T(8,128)(2,1)S(1)}, u32[]{:S(2)}, u32[]{:S(2)}) collective-permute-start(bf16[128,512]{1,0:T(8,128)(2,1)S(1)} %get-tuple-element.58), channel_id=1, source_target_pairs={{0,2},{1,3},{2,0},{3,1},{4,6},{5,7},{6,4},{7,5},{8,10},{9,11},{10,... | collective-permute-start | bytes 393224 | tf_op jit(solution)/shard_map/ppermute | solution.py:421
  168.0 5.4 %collective-permute-start.10 = (bf16[128,512]{1,0:T(8,128)(2,1)S(1)}, bf16[128,512]{1,0:T(8,128)(2,1)S(1)}, u32[]{:S(2)}, u32[]{:S(2)}) collective-permute-start(bf16[128,512]{1,0:T(8,128)(2,1)S(1)} %get-tuple-element.59), channel_id=1, source_target_pairs={{0,8},{1,9},{2,10},{3,11},{4,12},{5,13},{6,14},{7,15},{8,0},{9,1},... | collective-permute-start | bytes 393224 | tf_op jit(solution)/shard_map/ppermute | solution.py:421
  173.5 5.1 %collective-permute-start.12 = (bf16[128,512]{1,0:T(8,128)(2,1)S(1)}, bf16[128,512]{1,0:T(8,128)(2,1)S(1)}, u32[]{:S(2)}, u32[]{:S(2)}) collective-permute-start(bf16[128,512]{1,0:T(8,128)(2,1)S(1)} %add_convert_fusion.2), channel_id=1, source_target_pairs={{0,24},{1,25},{2,26},{3,27},{4,28},{5,29},{6,30},{7,31},{8,16},{9,... | collective-permute-start | bytes 393224 | tf_op jit(solution)/shard_map/ppermute | solution.py:421
  175.3 5.3 %collective-permute-start.13 = (bf16[128,512]{1,0:T(8,128)(2,1)S(1)}, bf16[128,512]{1,0:T(8,128)(2,1)S(1)}, u32[]{:S(2)}, u32[]{:S(2)}) collective-permute-start(bf16[128,512]{1,0:T(8,128)(2,1)S(1)} %add_convert_fusion), channel_id=1, source_target_pairs={{0,6},{1,7},{2,4},{3,5},{4,2},{5,3},{6,0},{7,1},{8,14},{9,15},{10,... | collective-permute-start | bytes 393224 | tf_op jit(solution)/shard_map/ppermute | solution.py:421
  180.7 5.9 %collective-permute-start.14 = (f32[2,128,512]{2,1,0:T(8,128)S(1)}, f32[2,128,512]{2,1,0:T(8,128)S(1)}, u32[]{:S(2)}, u32[]{:S(2)}) collective-permute-start(f32[2,128,512]{2,1,0:T(8,128)S(1)} %pad_maximum_fusion.2), channel_id=1, source_target_pairs={{0,1},{1,0},{2,3},{3,2},{4,5},{5,4},{6,7},{7,6},{8,9},{9,8},{10,11... | collective-permute-start | bytes 1572872 | tf_op jit(solution)/shard_map/ppermute | solution.py:498
